TPU v7x, 256 devices: a whole 4x4x8 slice. The times are simulated.
256 devices in a mesh: req: 32 (over z, x), tp: 8 (over y, core).
Axes of the slice: x: 4, y: 4, z: 8, core: 2. Of those that a mesh axis runs over, the one named last changes fastest.
Arguments:
- queries: bfloat16 [2048, 7168], P('req', 'tp'), may hold values from -8 to 8
- resident_kv: bfloat16 [6144, 64, 2048], P('req', None, 'tp'), may hold values from -8 to 8
- swap_kv: bfloat16 [1024, 64, 2048], P('req', None, 'tp'), may hold values from -8 to 8
- page_table: int32 [2048, 4], P('req'), may hold values from 0 to 255, as said below
- lengths: int32 [2048], P('req'), may hold values from 65 to 256, as said below
- resume_source: int32 [2048, 1], replicated, may hold values from 0 to 31; in each aligned block of 64 rows (0 to 63, 64 to 127, ...) at most 4 rows name the same one
- resume_page: int32 [2048], replicated, may hold values from 0 to 31
- seg_lengths: int32 [32, 32], P('req'), may hold values from 1 to 4, 64 in all within a row
- segment_adapter_holder: int32 [1024, 1], replicated, may hold values from 0 to 31; in each aligned block of 32 rows (0 to 31, 32 to 63, ...) at most 2 rows name the same one
- seg_slot: int32 [1024], replicated, may hold values from 0 to 15
- adapter_down: bfloat16 [512, 64, 7168], P('req', None, 'tp'), may hold values from -0.0625 to 0.0625
- adapter_up: bfloat16 [512, 64, 7168], P('req', None, 'tp'), may hold values from -0.75 to 0.75
Outputs:
- attention: bfloat16 [2048, 7168], P('req', 'tp')
- adapter_delta: bfloat16 [2048, 7168], P('req', 'tp')
- arrived_pages: bfloat16 [2048, 64, 2048], P('req', None, 'tp')
Inputs may be any that keep to these rules, and one draw needn't show every extreme that they name: `page_table`: within each block of 64 rows every number of 0 to 255 stands exactly once; numbers under 192 name the block's resident pages, 192 + j names the block's j-th resumed page. `lengths`: some request holds exactly 256 tokens. `resume_source`: rows come in blocks of 64, one block for each index of req in order; within one block no value stands more than 4 times. `seg_lengths`: each row sums to 64. `segment_adapter_holder`: rows come in blocks of 32, one block for each index of req in order; within one block no value stands more than 2 times.
All inputs are finite; a program needn't handle non-finite values.
Results may differ from a plain program's by a relative error of at most 0.011.
Values may be sent and summed in bfloat16 or wider, within the bound.
A program may use at most 128 MiB of HBM per device.

v0:
```python
import jax
import jax.numpy as jnp
from jax import lax
from jax.sharding import PartitionSpec as P

HD = 128
SEGMAX = 4


low_rank_scale = 2.0


def earlier_same(owner_ids, devices):
    marks = (owner_ids[:, :, None] == jnp.arange(devices, dtype=jnp.int32)[None, None, :]).astype(
        jnp.int32
    )
    before = jnp.cumsum(marks, axis=1) - marks
    return jnp.sum(before * marks, axis=2)


def pack_table(owner_ids, owner_rank, entries, source, capacity):
    places = jnp.arange(capacity, dtype=jnp.int32)
    matches = (owner_ids == source)[:, :, None] & (owner_rank[:, :, None] == places[None, None, :])
    return jnp.sum(jnp.where(matches, entries[:, :, None], 0), axis=1)


def attend(queries, page_space, req_table, req_lengths):
    req_count, width = queries.shape
    kv_heads = page_space.shape[2] // (2 * HD)
    group_size = width // (kv_heads * HD)
    positions = req_table.shape[1] * page_space.shape[1]
    picked = page_space[req_table].reshape(req_count, positions, kv_heads, 2, HD)
    head_rows = queries.reshape(req_count, kv_heads, group_size, HD)
    scores = jnp.einsum(
        "rkgd,rtkd->rkgt", head_rows, picked[:, :, :, 0, :], preferred_element_type=jnp.float32
    ) * HD ** (-0.5)
    live_mask = jnp.arange(positions, dtype=jnp.int32)[None, :] < req_lengths[:, None]
    scores = jnp.where(live_mask[:, None, None, :], scores, -1e30)
    row_top = jnp.max(scores, axis=-1, keepdims=True)
    weights = jnp.exp(scores - row_top)
    probabilities = (weights / jnp.sum(weights, axis=-1, keepdims=True)).astype(jnp.bfloat16)
    mixed = jnp.einsum(
        "rkgt,rtkd->rkgd", probabilities, picked[:, :, :, 1, :], preferred_element_type=jnp.float32
    )
    return mixed.reshape(req_count, width).astype(jnp.bfloat16)


def local(
    queries,
    resident_kv,
    swap_kv,
    page_table,
    lengths,
    resume_source,
    resume_page,
    seg_lengths,
    segment_adapter_holder,
    seg_slot,
    adapter_down,
    adapter_up,
):
    devices = lax.axis_size("req")
    own_index = lax.axis_index("req")
    req_count = queries.shape[0]
    res_rows = resume_page.shape[0] // devices
    res_cap = max(2, 2 * res_rows // devices)
    res_owner = resume_source[:, 0].reshape(devices, res_rows)
    res_rank = earlier_same(res_owner, devices)
    send_page = pack_table(
        res_owner, res_rank, resume_page.reshape(devices, res_rows), own_index, res_cap
    )
    arriving = lax.all_to_all(swap_kv[send_page], "req", split_axis=0, concat_axis=0, tiled=True)
    my_res_owner = lax.dynamic_index_in_dim(res_owner, own_index, 0, keepdims=False)
    my_res_rank = lax.dynamic_index_in_dim(res_rank, own_index, 0, keepdims=False)
    arrived = arriving.reshape((devices * res_cap,) + arriving.shape[2:])[
        my_res_owner * res_cap + my_res_rank
    ]
    page_space = jnp.concatenate([resident_kv, arrived], 0)
    mixed = attend(queries, page_space, page_table, lengths)
    segs = seg_lengths.shape[1]
    sizes_row = seg_lengths[0]
    seg_ends = jnp.cumsum(sizes_row)
    seg_starts = seg_ends - sizes_row
    positions = jnp.arange(req_count, dtype=jnp.int32)
    member = jnp.sum((positions[:, None] >= seg_ends[None, :]).astype(jnp.int32), axis=1)
    within = positions - seg_starts[member]
    offsets = jnp.arange(SEGMAX, dtype=jnp.int32)
    rows_per_block = jnp.minimum(seg_starts[:, None] + offsets[None, :], req_count - 1)
    filled = offsets[None, :] < sizes_row[:, None]
    blocks = jnp.where(filled[:, :, None], mixed[rows_per_block], jnp.zeros((), jnp.bfloat16))
    seg_cap = max(2, 2 * segs // devices)
    owners = segment_adapter_holder[:, 0].reshape(devices, segs)
    owner_rank = earlier_same(owners, devices)
    slots_all = seg_slot.reshape(devices, segs)
    my_owner = lax.dynamic_index_in_dim(owners, own_index, 0, keepdims=False)
    my_rank = lax.dynamic_index_in_dim(owner_rank, own_index, 0, keepdims=False)
    send_slot = pack_table(owners, owner_rank, slots_all, own_index, seg_cap)
    down_in, up_in = (
        lax.all_to_all(adapter_down[send_slot], "req", split_axis=0, concat_axis=0, tiled=True),
        lax.all_to_all(adapter_up[send_slot], "req", split_axis=0, concat_axis=0, tiled=True),
    )
    seg_pick = my_owner * seg_cap + my_rank
    down_seg = down_in.reshape((devices * seg_cap,) + down_in.shape[2:])[seg_pick]
    segment_up_weight = up_in.reshape((devices * seg_cap,) + up_in.shape[2:])[seg_pick]
    partial_sums = jnp.einsum("kmh,krh->kmr", blocks, down_seg, preferred_element_type=jnp.float32)
    down_projected = lax.psum(partial_sums, "tp").astype(jnp.bfloat16)
    delta_blocks = (
        jnp.einsum(
            "spw,swv->spv", down_projected, segment_up_weight, preferred_element_type=jnp.float32
        )
        * low_rank_scale
    ).astype(jnp.bfloat16)
    adapter_increment = delta_blocks.reshape(segs * SEGMAX, -1)[member * SEGMAX + within]
    return (mixed, adapter_increment, arrived)


def solution(mesh):
    return jax.shard_map(
        local,
        mesh=mesh,
        in_specs=(
            P("req", "tp"),
            P("req", None, "tp"),
            P("req", None, "tp"),
            P("req", None),
            P("req"),
            P(),
            P(),
            P("req", None),
            P(),
            P(),
            P("req", None, "tp"),
            P("req", None, "tp"),
        ),
        out_specs=(P("req", "tp"), P("req", "tp"), P("req", None, "tp")),
        check_vma=False,
    )
```

profile of v0, /device:TPU:1, one launch (start us, length us, event | category | flops | bytes accessed | tf_op | source)
XLA Modules:
  0.0 479.3 jit_solution(17246039470363001393)
XLA Ops:
  0.6 0.0 copy-start
  0.7 0.5 broadcast.304
  1.2 1.4 reduce.15
  2.6 0.1 reshape_squeeze.6
  2.6 0.1 copy.54
  2.7 1.7 select_reduce_fusion
  4.5 0.1 copy.55
  4.5 0.8 broadcast_in_dim.51
  5.3 0.1 select_reduce_fusion.1
  5.5 0.1 copy.56
  5.5 0.1 reshape.329
  5.7 4.1 gather_fusion
  9.8 12.1 %all-to-all-start = ((bf16[32,4,64,256]{3,2,1,0:T(8,128)(2,1)}), bf16[32,4,64,256]{3,2,1,0:T(8,128)(2,1)}, u32[]{:S(2)}, u32[]{:S(2)}) async-start(bf16[32,4,64,256]{3,2,1,0:T(8,128)(2,1)} %bitcast.76), calls=%async_computation | async-start | bytes 8388608 | tf_op jit(solution)/shard_map/all_to_all | solution.py:72
  21.9 0.0 copy-done.6
  21.9 0.7 reduce.16
  22.6 0.1 reshape_squeeze.7
  22.6 0.1 copy.63
  22.7 1.0 fusion.34
  23.8 0.1 copy.64
  23.8 0.0 copy-done.5
  23.8 0.1 broadcast_in_dim.91
  23.9 0.1 select_reduce_fusion.2
  24.1 0.1 copy.65
  24.1 0.1 reshape.361
  24.3 0.0 copy-done
  24.3 4.3 gather_fusion.4
  28.6 86.3 %all-to-all-done = bf16[32,4,64,256]{3,2,1,0:T(8,128)(2,1)} async-done(((bf16[32,4,64,256]{3,2,1,0:T(8,128)(2,1)}), bf16[32,4,64,256]{3,2,1,0:T(8,128)(2,1)}, u32[]{:S(2)}, u32[]{:S(2)}) %all-to-all-start) | async-done | bytes 4194336 | tf_op jit(solution)/shard_map/all_to_all | solution.py:72
  114.9 8.5 %all-to-all-start.1 = ((bf16[32,2,64,896]{3,2,1,0:T(8,128)(2,1)}), bf16[32,2,64,896]{3,2,1,0:T(8,128)(2,1)}, u32[]{:S(2)}, u32[]{:S(2)}) async-start(bf16[32,2,64,896]{3,2,1,0:T(8,128)(2,1)} %bitcast.75), calls=%async_computation.1 | async-start | bytes 14680064 | tf_op jit(solution)/shard_map/all_to_all | solution.py:99
  123.5 4.3 gather_fusion.6
  127.8 160.3 %all-to-all-done.1 = bf16[32,2,64,896]{3,2,1,0:T(8,128)(2,1)} async-done(((bf16[32,2,64,896]{3,2,1,0:T(8,128)(2,1)}), bf16[32,2,64,896]{3,2,1,0:T(8,128)(2,1)}, u32[]{:S(2)}, u32[]{:S(2)}) %all-to-all-start.1) | async-done | bytes 7340064 | tf_op jit(solution)/shard_map/all_to_all | solution.py:99
  288.1 15.0 %all-to-all-start.2 = ((bf16[32,2,64,896]{3,2,1,0:T(8,128)(2,1)}), bf16[32,2,64,896]{3,2,1,0:T(8,128)(2,1)}, u32[]{:S(2)}, u32[]{:S(2)}) async-start(bf16[32,2,64,896]{3,2,1,0:T(8,128)(2,1)} %bitcast.74), calls=%async_computation.2 | async-start | bytes 14680064 | tf_op jit(solution)/shard_map/all_to_all | solution.py:100
  303.2 0.1 copy.58
  303.3 0.1 reshape.345
  303.4 0.2 reshape.320
  303.6 0.0 copy-done.7
  303.6 0.1 copy.61
  303.6 0.1 reduce-window.7
  303.7 0.1 reduce.6
  303.8 0.1 copy.62
  303.9 0.1 reshape.353
  304.0 0.1 convert_reduce_fusion
  304.2 0.8 gather_fusion.8
  304.9 0.2 add_reduce_fusion.1
  305.1 0.2 add_reduce_fusion
  305.4 0.1 iota_compare_fusion.8
  305.5 0.1 iota_compare_fusion.5
  305.6 4.2 gather_fusion.1
  309.8 7.4 %pad_maximum_fusion = bf16[256,64,256]{2,1,0:T(8,128)(2,1)} fusion(bf16[64,64,256]{2,1,0:T(8,128)(2,1)} %gather_fusion.1, bf16[192,64,256]{2,1,0:T(8,128)(2,1)} %param.13), kind=kLoop, calls=%fused_computation.11 | loop fusion | flops 4194304 | bytes 16777216 | tf_op jit(solution)/shard_map/concatenate | solution.py:78
  317.1 12.0 %gather_fusion.2 = bf16[256,64,256]{2,1,0:T(8,128)(2,1)} fusion(bf16[256,64,256]{2,1,0:T(8,128)(2,1)} %pad_maximum_fusion, s32[1024]{0:T(1024)S(1)} %pad_clamp_fusion.5), kind=kCustom, calls=%fused_computation.2 | custom fusion | bytes 16778240 | tf_op jit(solution)/shard_map/gather | solution.py:32
  329.1 12.5 %reshape.318 = bf16[64,256,1,2,128]{4,3,1,0,2:T(2,128)(2,1)} reshape(bf16[256,64,256]{2,1,0:T(8,128)(2,1)} %gather_fusion.2) | data formatting | bytes 16777216 | tf_op jit(solution)/shard_map/reshape | solution.py:32
  341.7 17.5 %fusion.32 = (bf16[64,256,1,1,128]{4,3,1,0,2:T(2,128)(2,1)}, bf16[64,256,1,1,128]{4,3,1,0,2:T(2,128)(2,1)}) fusion(bf16[64,256,1,2,128]{4,3,1,0,2:T(2,128)(2,1)} %reshape.318), kind=kLoop, calls=%fused_computation.82 | loop fusion | bytes 16777216 | tf_op jit(solution)/shard_map/slice | solution.py:35
  359.2 4.7 fusion.33
  363.9 4.1 fusion.13
  368.1 0.0 copy-start.2
  368.1 0.9 gather_fusion.3
  369.0 0.1 reshape.352
  369.0 5.8 %gather_fusion.5 = bf16[32,64,896]{2,1,0:T(8,128)(2,1)} fusion(bf16[64,64,896]{2,1,0:T(8,128)(2,1)} %bitcast.11, s32[1024]{0:T(1024)S(1)} %pad_clamp_fusion.2), kind=kCustom, calls=%fused_computation.5 | custom fusion | bytes 7340160 | tf_op jit(solution)/shard_map/gather | solution.py:103
  374.9 3.3 fusion.19
  378.1 24.7 %psum.7 = bf16[32,4,64]{2,1,0:T(4,128)(2,1)S(1)} all-reduce(f32[32,4,64]{2,1,0:T(4,128)S(1)} %fusion.19), channel_id=1, replica_groups=mesh['req'=32,'tp'=8] {'tp'}, use_global_device_ids=true, to_apply=%region_9.10 | all-reduce | flops 8192 | bytes 49152 | tf_op jit(solution)/shard_map/psum | solution.py:106
  402.8 66.4 %all-to-all-done.2 = bf16[32,2,64,896]{3,2,1,0:T(8,128)(2,1)} async-done(((bf16[32,2,64,896]{3,2,1,0:T(8,128)(2,1)}), bf16[32,2,64,896]{3,2,1,0:T(8,128)(2,1)}, u32[]{:S(2)}, u32[]{:S(2)}) %all-to-all-start.2) | async-done | bytes 7340064 | tf_op jit(solution)/shard_map/all_to_all | solution.py:100
  469.2 6.0 %gather_fusion.7 = bf16[32,64,896]{2,1,0:T(8,128)(2,1)} fusion(bf16[64,64,896]{2,1,0:T(8,128)(2,1)} %bitcast.14, s32[1024]{0:T(1024)S(1)} %pad_clamp_fusion.2), kind=kCustom, calls=%fused_computation.7 | custom fusion | bytes 7340160 | tf_op jit(solution)/shard_map/gather | solution.py:104
  475.2 2.7 fusion.10
  477.9 0.1 reshape.326
  477.9 1.4 gather_fusion.9
  (34 shorter events, 0.2 us)
Async XLA Ops:
  0.6 23.6 %copy-start = (bf16[16,64,896]{2,1,0:T(8,128)(2,1)S(1)}, bf16[16,64,896]{2,1,0:T(8,128)(2,1)}, u32[]{:S(2)}) copy-start(bf16[16,64,896]{2,1,0:T(8,128)(2,1)} %param.22) | copy-start | bytes 5505028
  9.8 12.1 %copy-start.6 = (s32[1024,1]{0,1:T(1,128)S(1)}, s32[1024,1]{0,1:T(1,128)}, u32[]{:S(2)}) copy-start(s32[1024,1]{0,1:T(1,128)} %param.20) | copy-start | bytes 12292
  9.8 14.1 %copy-start.5 = (s32[1024]{0:T(1024)S(1)}, s32[1024]{0:T(1024)}, u32[]{:S(2)}) copy-start(s32[1024]{0:T(1024)} %param.21) | copy-start | bytes 12292
  9.8 105.2 %all-to-all-start = ((bf16[32,4,64,256]{3,2,1,0:T(8,128)(2,1)}), bf16[32,4,64,256]{3,2,1,0:T(8,128)(2,1)}, u32[]{:S(2)}, u32[]{:S(2)}) async-start(bf16[32,4,64,256]{3,2,1,0:T(8,128)(2,1)} %bitcast.76), calls=%async_computation | async-start | bytes 8388608 | tf_op jit(solution)/shard_map/all_to_all | solution.py:72
  114.9 8.5 %copy-start.3 = (bf16[16,64,896]{2,1,0:T(8,128)(2,1)S(1)}, bf16[16,64,896]{2,1,0:T(8,128)(2,1)}, u32[]{:S(2)}) copy-start(bf16[16,64,896]{2,1,0:T(8,128)(2,1)} %param.23) | copy-start | bytes 5505028
  114.9 173.2 %all-to-all-start.1 = ((bf16[32,2,64,896]{3,2,1,0:T(8,128)(2,1)}), bf16[32,2,64,896]{3,2,1,0:T(8,128)(2,1)}, u32[]{:S(2)}, u32[]{:S(2)}) async-start(bf16[32,2,64,896]{3,2,1,0:T(8,128)(2,1)} %bitcast.75), calls=%async_computation.1 | async-start | bytes 14680064 | tf_op jit(solution)/shard_map/all_to_all | solution.py:99
  288.1 15.1 %copy-start.8 = (s32[64,4]{0,1:T(4,128)S(1)}, s32[64,4]{0,1:T(4,128)}, u32[]{:S(2)}) copy-start(s32[64,4]{0,1:T(4,128)} %param.15) | copy-start | bytes 3076
  288.1 15.3 %copy-start.4 = (bf16[64,896]{1,0:T(8,128)(2,1)S(1)}, bf16[64,896]{1,0:T(8,128)(2,1)}, u32[]{:S(2)}) copy-start(bf16[64,896]{1,0:T(8,128)(2,1)} %param.12) | copy-start | bytes 344068
  288.1 15.4 %copy-start.7 = (s32[1,32]{1,0:T(1,128)S(1)}, s32[1,32]{1,0:T(1,128)}, u32[]{:S(2)}) copy-start(s32[1,32]{1,0:T(1,128)} %param.19) | copy-start | bytes 388
  288.1 17.4 %copy-start.9 = (s32[64]{0:T(128)S(1)}, s32[64]{0:T(128)}, u32[]{:S(2)}) copy-start(s32[64]{0:T(128)} %param.16) | copy-start | bytes 772
  288.1 181.1 %all-to-all-start.2 = ((bf16[32,2,64,896]{3,2,1,0:T(8,128)(2,1)}), bf16[32,2,64,896]{3,2,1,0:T(8,128)(2,1)}, u32[]{:S(2)}, u32[]{:S(2)}) async-start(bf16[32,2,64,896]{3,2,1,0:T(8,128)(2,1)} %bitcast.74), calls=%async_computation.2 | async-start | bytes 14680064 | tf_op jit(solution)/shard_map/all_to_all | solution.py:100
  368.1 10.1 %copy-start.2 = (bf16[8,8,7,128]{3,1,2,0:T(8,128)(2,1)}, bf16[8,8,7,128]{3,1,2,0:T(8,128)(2,1)S(1)}, u32[]{:S(2)}) copy-start(bf16[8,8,7,128]{3,1,2,0:T(8,128)(2,1)S(1)} %copy.85) | copy-start | bytes 344068
  469.2 10.1 %copy-start.1 = (bf16[16,64,896]{2,1,0:T(8,128)(2,1)S(1)}, bf16[16,64,896]{2,1,0:T(8,128)(2,1)}, u32[]{:S(2)}) copy-start(bf16[16,64,896]{2,1,0:T(8,128)(2,1)} %param.22) | copy-start | bytes 5505028
where the time goes:
time: 482 us; the launch traced here: 479 us
  waiting for transfers between devices  313 us (65%)
  local copies, waits for them, and re-layouts  76.8 us (16%)
  starting transfers between devices  35.7 us (7%)
  blocking collectives  24.7 us (5%)
  matrix products  14.8 us (3%)
  other arithmetic  13.4 us (3%)
    all_to_all x1, waiting for transfers between devices, local(): lax.all_to_all(adapter_down[send_slot], 'req', split_axis=0, concat_axis=...  160 us
    all_to_all x1, waiting for transfers between devices, local(): lax.all_to_all(swap_kv[send_page], 'req', split_axis=0, concat_axis=0, ti...  86.3 us
    all_to_all x1, waiting for transfers between devices, local(): lax.all_to_all(adapter_up[send_slot], 'req', split_axis=0, concat_axis=0,...  66.4 us
    psum x1, blocking collectives, local(): down_projected = lax.psum(partial_sums, 'tp').astype(jnp.bfloat16)  24.7 us
    slice x1, local copies, waits for them, and re-layouts, attend(): picked[:, :, :, 0, :]  17.5 us
    all_to_all x1, starting transfers between devices, local(): lax.all_to_all(adapter_up[send_slot], 'req', split_axis=0, concat_axis=0,...  15 us
    reshape x1, local copies, waits for them, and re-layouts, attend(): page_space[req_table].reshape(req_count, positions, kv_heads, 2, HD)  12.5 us
    all_to_all x1, starting transfers between devices, local(): lax.all_to_all(swap_kv[send_page], 'req', split_axis=0, concat_axis=0, ti...  12.1 us
  transfers between devices with their start and end apart: 3, of which 3 were waited for; matrix products, arithmetic and copies ran while one was open for 18% of the time, Pallas kernels for 0%

commit v1 on v0

--- a/solution.py
+++ b/solution.py
@@ -78,39 +78,49 @@
     page_space = jnp.concatenate([resident_kv, arrived], 0)
     mixed = attend(queries, page_space, page_table, lengths)
     segs = seg_lengths.shape[1]
+    rank = adapter_down.shape[1]
+    slots = adapter_down.shape[0]
+    width = queries.shape[1]
     sizes_row = seg_lengths[0]
     seg_ends = jnp.cumsum(sizes_row)
     seg_starts = seg_ends - sizes_row
     positions = jnp.arange(req_count, dtype=jnp.int32)
     member = jnp.sum((positions[:, None] >= seg_ends[None, :]).astype(jnp.int32), axis=1)
     within = positions - seg_starts[member]
-    offsets = jnp.arange(SEGMAX, dtype=jnp.int32)
-    rows_per_block = jnp.minimum(seg_starts[:, None] + offsets[None, :], req_count - 1)
-    filled = offsets[None, :] < sizes_row[:, None]
-    blocks = jnp.where(filled[:, :, None], mixed[rows_per_block], jnp.zeros((), jnp.bfloat16))
     seg_cap = max(2, 2 * segs // devices)
     owners = segment_adapter_holder[:, 0].reshape(devices, segs)
     owner_rank = earlier_same(owners, devices)
     slots_all = seg_slot.reshape(devices, segs)
     my_owner = lax.dynamic_index_in_dim(owners, own_index, 0, keepdims=False)
     my_rank = lax.dynamic_index_in_dim(owner_rank, own_index, 0, keepdims=False)
-    send_slot = pack_table(owners, owner_rank, slots_all, own_index, seg_cap)
-    down_in, up_in = (
-        lax.all_to_all(adapter_down[send_slot], "req", split_axis=0, concat_axis=0, tiled=True),
-        lax.all_to_all(adapter_up[send_slot], "req", split_axis=0, concat_axis=0, tiled=True),
+    held_slot = pack_table(owners, owner_rank, slots_all, own_index, seg_cap)
+    place = ((my_owner * seg_cap + my_rank)[member]) * SEGMAX + within
+    rows_out = devices * seg_cap * SEGMAX
+    put = (jnp.arange(rows_out, dtype=jnp.int32)[:, None] == place[None, :]).astype(jnp.bfloat16)
+    rows = jnp.dot(put, mixed, preferred_element_type=jnp.float32).astype(jnp.bfloat16)
+    rows = lax.all_to_all(
+        rows.reshape(devices, seg_cap * SEGMAX, width), "req", split_axis=0, concat_axis=0, tiled=True
+    ).reshape(rows_out, width)
+    row_slot = jnp.repeat(held_slot.reshape(-1), SEGMAX)
+    pick = row_slot[:, None] == jnp.arange(slots, dtype=jnp.int32)[None, :]
+    shrunk = jnp.einsum(
+        "nh,srh->nsr", rows, adapter_down, preferred_element_type=jnp.float32
     )
-    seg_pick = my_owner * seg_cap + my_rank
-    down_seg = down_in.reshape((devices * seg_cap,) + down_in.shape[2:])[seg_pick]
-    segment_up_weight = up_in.reshape((devices * seg_cap,) + up_in.shape[2:])[seg_pick]
-    partial_sums = jnp.einsum("kmh,krh->kmr", blocks, down_seg, preferred_element_type=jnp.float32)
-    down_projected = lax.psum(partial_sums, "tp").astype(jnp.bfloat16)
-    delta_blocks = (
-        jnp.einsum(
-            "spw,swv->spv", down_projected, segment_up_weight, preferred_element_type=jnp.float32
+    shrunk = jnp.sum(jnp.where(pick[:, :, None], shrunk, 0.0), axis=1)
+    shrunk = lax.psum(shrunk, "tp").astype(jnp.bfloat16)
+    spread = jnp.where(pick[:, :, None], shrunk[:, None, :], jnp.zeros((), jnp.bfloat16))
+    delta = (
+        jnp.dot(
+            spread.reshape(rows_out, slots * rank),
+            adapter_up.reshape(slots * rank, width),
+            preferred_element_type=jnp.float32,
         )
         * low_rank_scale
     ).astype(jnp.bfloat16)
-    adapter_increment = delta_blocks.reshape(segs * SEGMAX, -1)[member * SEGMAX + within]
+    back = lax.all_to_all(
+        delta.reshape(devices, seg_cap * SEGMAX, width), "req", split_axis=0, concat_axis=0, tiled=True
+    ).reshape(rows_out, width)
+    adapter_increment = back[place]
     return (mixed, adapter_increment, arrived)
 
 

time: 482 us -> 253 us (0.52)
  the two profiles are of different devices: /device:TPU:1 before, /device:TPU:24 now
where the time goes in v1:
time: 253 us; the launch traced here: 252 us
  waiting for transfers between devices  123 us (49%)
  local copies, waits for them, and re-layouts  56 us (22%)
  starting transfers between devices  23.7 us (9%)
  blocking collectives  21.3 us (8%)
  matrix products  13.7 us (5%)
  other arithmetic  13.3 us (5%)
    all_to_all x1, waiting for transfers between devices, local(): lax.all_to_all(swap_kv[send_page], 'req', split_axis=0, concat_axis=0, ti...  89.6 us
    psum x1, blocking collectives, local(): shrunk = lax.psum(shrunk, 'tp').astype(jnp.bfloat16)  21.3 us
    slice x1, local copies, waits for them, and re-layouts, attend(): picked[:, :, :, 0, :]  17.5 us
    all_to_all x1, waiting for transfers between devices, local(): lax.all_to_all(delta.reshape(devices, seg_cap * SEGMAX, width), 'req', sp...  17.4 us
    all_to_all x1, waiting for transfers between devices, local(): lax.all_to_all(rows.reshape(devices, seg_cap * SEGMAX, width), 'req', spl...  16 us
    reshape x1, local copies, waits for them, and re-layouts, attend(): page_space[req_table].reshape(req_count, positions, kv_heads, 2, HD)  12.5 us
    gather x1, local copies, waits for them, and re-layouts, attend(): page_space[req_table].reshape(req_count, positions, kv_heads, 2, HD)  12 us
    all_to_all x1, starting transfers between devices, local(): lax.all_to_all(swap_kv[send_page], 'req', split_axis=0, concat_axis=0, ti...  11.6 us
  transfers between devices with their start and end apart: 3, of which 3 were waited for; matrix products, arithmetic and copies ran while one was open for 2% of the time, Pallas kernels for 0%

profile of v1, /device:TPU:24, one launch (start us, length us, event | category | flops | bytes accessed | tf_op | source)
XLA Modules:
  0.0 252.0 jit_solution(1999964217303463869)
XLA Ops:
  0.6 0.0 copy-start
  0.6 0.5 broadcast.190
  1.2 1.4 reduce.15
  2.6 0.1 reshape_squeeze.6
  2.6 0.1 copy.46
  2.7 1.7 select_reduce_fusion
  4.5 0.1 copy.47
  4.5 0.8 broadcast_in_dim.103
  5.3 0.1 select_reduce_fusion.1
  5.5 0.1 copy.48
  5.5 0.1 reshape.266
  5.7 4.0 %gather_fusion = bf16[128,64,256]{2,1,0:T(8,128)(2,1)} fusion(bf16[32,64,256]{2,1,0:T(8,128)(2,1)} %param.14, s32[1024]{0:T(1024)S(1)} %pad_clamp_fusion.4), kind=kCustom, calls=%fused_computation | custom fusion | bytes 8389120 | tf_op jit(solution)/shard_map/gather | solution.py:72
  9.7 0.0 copy-start.5
  9.7 0.0 copy-start.7
  9.7 11.6 %all-to-all-start = ((bf16[32,4,64,256]{3,2,1,0:T(8,128)(2,1)}), bf16[32,4,64,256]{3,2,1,0:T(8,128)(2,1)}, u32[]{:S(2)}, u32[]{:S(2)}) async-start(bf16[32,4,64,256]{3,2,1,0:T(8,128)(2,1)} %bitcast.75), calls=%async_computation | async-start | bytes 8388608 | tf_op jit(solution)/shard_map/all_to_all | solution.py:72
  21.3 0.0 copy-done.5
  21.3 0.1 copy.50
  21.4 0.1 reshape.282
  21.5 0.0 copy-done.2
  21.5 0.2 reshape.255
  21.7 0.0 copy-done.4
  21.7 0.7 reduce.16
  22.4 0.1 reshape_squeeze.7
  22.4 0.1 copy.53
  22.5 0.0 copy-done.6
  22.5 0.1 copy.57
  22.6 0.1 reduce-window.8
  22.7 0.1 reduce.8
  22.8 1.0 fusion.38
  23.8 0.2 add_reduce_fusion.1
  24.0 0.1 convert_reduce_fusion
  24.1 0.8 gather_fusion.3
  24.9 0.8 gather_fusion.4
  25.7 0.2 add_reduce_fusion
  25.9 0.0 copy-done.7
  25.9 0.1 iota_compare_fusion.7
  26.0 89.6 %all-to-all-done = bf16[32,4,64,256]{3,2,1,0:T(8,128)(2,1)} async-done(((bf16[32,4,64,256]{3,2,1,0:T(8,128)(2,1)}), bf16[32,4,64,256]{3,2,1,0:T(8,128)(2,1)}, u32[]{:S(2)}, u32[]{:S(2)}) %all-to-all-start) | async-done | bytes 4194336 | tf_op jit(solution)/shard_map/all_to_all | solution.py:72
  115.6 4.2 %gather_fusion.1 = bf16[64,64,256]{2,1,0:T(8,128)(2,1)} fusion(bf16[128,64,256]{2,1,0:T(8,128)(2,1)} %bitcast.2, s32[1024]{0:T(1024)S(1)} %pad_clamp_fusion.3), kind=kCustom, calls=%fused_computation.1 | custom fusion | bytes 4194560 | tf_op jit(solution)/shard_map/gather | solution.py:75
  119.8 7.4 %pad_maximum_fusion = bf16[256,64,256]{2,1,0:T(8,128)(2,1)} fusion(bf16[64,64,256]{2,1,0:T(8,128)(2,1)} %gather_fusion.1, bf16[192,64,256]{2,1,0:T(8,128)(2,1)} %param.13), kind=kLoop, calls=%fused_computation.7 | loop fusion | flops 4194304 | bytes 16777216 | tf_op jit(solution)/shard_map/concatenate | solution.py:78
  127.2 12.0 %gather_fusion.2 = bf16[256,64,256]{2,1,0:T(8,128)(2,1)} fusion(bf16[256,64,256]{2,1,0:T(8,128)(2,1)} %pad_maximum_fusion, s32[1024]{0:T(1024)S(1)} %pad_clamp_fusion.2), kind=kCustom, calls=%fused_computation.2 | custom fusion | bytes 16778240 | tf_op jit(solution)/shard_map/gather | solution.py:32
  139.2 12.5 %reshape.253 = bf16[64,256,1,2,128]{4,3,1,0,2:T(2,128)(2,1)} reshape(bf16[256,64,256]{2,1,0:T(8,128)(2,1)} %gather_fusion.2) | data formatting | bytes 16777216 | tf_op jit(solution)/shard_map/reshape | solution.py:32
  151.7 17.5 %fusion.36 = (bf16[64,256,1,1,128]{4,3,1,0,2:T(2,128)(2,1)}, bf16[64,256,1,1,128]{4,3,1,0,2:T(2,128)(2,1)}) fusion(bf16[64,256,1,2,128]{4,3,1,0,2:T(2,128)(2,1)} %reshape.253), kind=kLoop, calls=%fused_computation.79 | loop fusion | bytes 16777216 | tf_op jit(solution)/shard_map/slice | solution.py:35
  169.3 4.7 %fusion.37 = (f32[64,7]{1,0:T(8,128)S(1)}, f32[64,7,256]{2,1,0:T(8,128)S(1)}) fusion(bf16[64,7,128]{2,1,0:T(8,128)(2,1)S(1)} %reshape.255, bf16[64,256,1,1,128]{4,3,1,0,2:T(2,128)(2,1)} %get-tuple-element.3, pred[64,256]{1,0:T(8,128)(4,1)S(1)} %iota_compare_fusion.7), kind=kOutput, calls=%fused_computation.80 | convolution fusion | flops 29819136 | bytes 4785920 | tf_op jit(solution)/shard_map/sub | solution.py:40
  174.0 4.1 %fusion.17 = bf16[64,7,128]{2,1,0:T(8,128)(2,1)S(1)} fusion(bf16[64,256,1,1,128]{4,3,1,0,2:T(2,128)(2,1)} %get-tuple-element.4, f32[64,7,256]{2,1,0:T(8,128)S(1)} %get-tuple-element.6, f32[64,7]{1,0:T(8,128)S(1)} %get-tuple-element.5), kind=kOutput, calls=%fused_computation.28 | convolution fusion | flops 29646848 | bytes 4769536 | tf_op jit(solution)/shard_map/rkgt,rtkd->rkgd/dot_general | solution.py:42
  178.2 0.0 copy-start.1
  178.2 1.0 fusion.13
  179.2 6.8 %all-to-all-start.1 = ((bf16[32,8,896]{2,1,0:T(8,128)(2,1)}), bf16[32,8,896]{2,1,0:T(8,128)(2,1)S(1)}, u32[]{:S(2)}, u32[]{:S(2)}) async-start(bf16[32,8,896]{2,1,0:T(8,128)(2,1)} %fusion.13), calls=%async_computation.1 | async-start | bytes 917504 | tf_op jit(solution)/shard_map/all_to_all | solution.py:101
  186.0 0.1 copy.54
  186.1 0.0 copy-done.3
  186.1 0.1 broadcast_in_dim.108
  186.1 0.1 select_reduce_fusion.2
  186.3 0.1 copy.55
  186.4 0.1 reshape.257
  186.5 0.1 broadcast_in_dim.111
  186.5 0.1 eq.120
  186.7 16.0 %all-to-all-done.1 = bf16[32,8,896]{2,1,0:T(8,128)(2,1)S(1)} async-done(((bf16[32,8,896]{2,1,0:T(8,128)(2,1)}), bf16[32,8,896]{2,1,0:T(8,128)(2,1)S(1)}, u32[]{:S(2)}, u32[]{:S(2)}) %all-to-all-start.1) | async-done | bytes 458784 | tf_op jit(solution)/shard_map/all_to_all | solution.py:101
  202.7 2.2 fusion.10
  205.0 21.3 %psum.7 = bf16[256,64]{0,1:T(8,128)(2,1)S(1)} all-reduce(f32[256,64]{0,1:T(8,128)S(1)} %fusion.10), channel_id=1, replica_groups=mesh['req'=32,'tp'=8] {'tp'}, use_global_device_ids=true, to_apply=%region_11.12 | all-reduce | flops 16384 | bytes 98304 | tf_op jit(solution)/shard_map/psum | solution.py:110
  226.3 0.0 copy-done
  226.3 1.5 fusion.14
  227.8 0.0 copy-done.1
  227.8 5.4 %all-to-all-start.2 = ((bf16[32,8,896]{2,1,0:T(8,128)(2,1)}), bf16[32,8,896]{2,1,0:T(8,128)(2,1)S(1)}, u32[]{:S(2)}, u32[]{:S(2)}) async-start(bf16[32,8,896]{2,1,0:T(8,128)(2,1)} %fusion.14), calls=%async_computation.2 | async-start | bytes 917504 | tf_op jit(solution)/shard_map/all_to_all | solution.py:120
  233.2 17.4 %all-to-all-done.2 = bf16[32,8,896]{2,1,0:T(8,128)(2,1)S(1)} async-done(((bf16[32,8,896]{2,1,0:T(8,128)(2,1)}), bf16[32,8,896]{2,1,0:T(8,128)(2,1)S(1)}, u32[]{:S(2)}, u32[]{:S(2)}) %all-to-all-start.2) | async-done | bytes 458784 | tf_op jit(solution)/shard_map/all_to_all | solution.py:120
  250.7 1.4 gather_fusion.5
  (20 shorter events, 0.1 us)
Async XLA Ops:
  0.6 225.7 %copy-start = (bf16[16,64,896]{2,1,0:T(8,128)(2,1)S(1)}, bf16[16,64,896]{2,1,0:T(8,128)(2,1)}, u32[]{:S(2)}) copy-start(bf16[16,64,896]{2,1,0:T(8,128)(2,1)} %param.23) | copy-start | bytes 5505028
  9.7 11.6 %copy-start.5 = (s32[64,4]{0,1:T(4,128)S(1)}, s32[64,4]{0,1:T(4,128)}, u32[]{:S(2)}) copy-start(s32[64,4]{0,1:T(4,128)} %param.15) | copy-start | bytes 3076
  9.7 11.8 %copy-start.2 = (bf16[64,896]{1,0:T(8,128)(2,1)S(1)}, bf16[64,896]{1,0:T(8,128)(2,1)}, u32[]{:S(2)}) copy-start(bf16[64,896]{1,0:T(8,128)(2,1)} %param.12) | copy-start | bytes 344068
  9.7 12.0 %copy-start.4 = (s32[1024,1]{0,1:T(1,128)S(1)}, s32[1024,1]{0,1:T(1,128)}, u32[]{:S(2)}) copy-start(s32[1024,1]{0,1:T(1,128)} %param.20) | copy-start | bytes 12292
  9.7 12.8 %copy-start.6 = (s32[1,32]{1,0:T(1,128)S(1)}, s32[1,32]{1,0:T(1,128)}, u32[]{:S(2)}) copy-start(s32[1,32]{1,0:T(1,128)} %param.19) | copy-start | bytes 388
  9.7 16.2 %copy-start.7 = (s32[64]{0:T(128)S(1)}, s32[64]{0:T(128)}, u32[]{:S(2)}) copy-start(s32[64]{0:T(128)} %param.16) | copy-start | bytes 772
  9.7 105.9 %all-to-all-start = ((bf16[32,4,64,256]{3,2,1,0:T(8,128)(2,1)}), bf16[32,4,64,256]{3,2,1,0:T(8,128)(2,1)}, u32[]{:S(2)}, u32[]{:S(2)}) async-start(bf16[32,4,64,256]{3,2,1,0:T(8,128)(2,1)} %bitcast.75), calls=%async_computation | async-start | bytes 8388608 | tf_op jit(solution)/shard_map/all_to_all | solution.py:72
  174.0 12.1 %copy-start.3 = (s32[1024]{0:T(1024)S(1)}, s32[1024]{0:T(1024)}, u32[]{:S(2)}) copy-start(s32[1024]{0:T(1024)} %param.21) | copy-start | bytes 12292
  178.2 49.7 %copy-start.1 = (bf16[8,8,7,128]{3,1,2,0:T(8,128)(2,1)}, bf16[8,8,7,128]{3,1,2,0:T(8,128)(2,1)S(1)}, u32[]{:S(2)}) copy-start(bf16[8,8,7,128]{3,1,2,0:T(8,128)(2,1)S(1)} %copy.76) | copy-start | bytes 344068
  179.2 23.5 %all-to-all-start.1 = ((bf16[32,8,896]{2,1,0:T(8,128)(2,1)}), bf16[32,8,896]{2,1,0:T(8,128)(2,1)S(1)}, u32[]{:S(2)}, u32[]{:S(2)}) async-start(bf16[32,8,896]{2,1,0:T(8,128)(2,1)} %fusion.13), calls=%async_computation.1 | async-start | bytes 917504 | tf_op jit(solution)/shard_map/all_to_all | solution.py:101
  227.8 22.8 %all-to-all-start.2 = ((bf16[32,8,896]{2,1,0:T(8,128)(2,1)}), bf16[32,8,896]{2,1,0:T(8,128)(2,1)S(1)}, u32[]{:S(2)}, u32[]{:S(2)}) async-start(bf16[32,8,896]{2,1,0:T(8,128)(2,1)} %fusion.14), calls=%async_computation.2 | async-start | bytes 917504 | tf_op jit(solution)/shard_map/all_to_all | solution.py:120

commit v2 on v0

v2 whole, which is shorter than its diff:
```python
import functools

import jax
import jax.numpy as jnp
from jax import lax
from jax.experimental import pallas as pl
from jax.experimental.pallas import tpu as pltpu
from jax.sharding import PartitionSpec as P

HD = 128
SEGMAX = 4
LANES = 128
MESH = pl.DeviceIdType.MESH
NEG = -1e30

low_rank_scale = 2.0


def earlier_same(owner_ids, devices):
    marks = (owner_ids[:, :, None] == jnp.arange(devices, dtype=jnp.int32)[None, None, :]).astype(
        jnp.int32
    )
    before = jnp.cumsum(marks, axis=1) - marks
    return jnp.sum(before * marks, axis=2)


def pack_table(owner_ids, owner_rank, entries, source, capacity):
    places = jnp.arange(capacity, dtype=jnp.int32)
    matches = (owner_ids == source)[:, :, None] & (owner_rank[:, :, None] == places[None, None, :])
    return jnp.sum(jnp.where(matches, entries[:, :, None], 0), axis=1)


def attend_kernel(
    pool, table, lens, place, q_ref, resident, recv, out_ref, arrived, space, qs, att, sem, asem
):
    reqs, width = q_ref.shape
    heads = width // HD
    page = space.shape[1]
    maxp = table.shape[0] // reqs
    span = maxp * page
    news = place.shape[0]
    load_a = pltpu.make_async_copy(resident, space.at[pl.ds(0, pool)], sem.at[0])
    load_b = pltpu.make_async_copy(recv, space.at[pl.ds(pool, recv.shape[0])], sem.at[1])
    load_a.start()
    load_b.start()
    qs[...] = jnp.zeros_like(qs)
    for h in range(heads):
        qs[pl.ds(h, reqs, stride=8), :] = q_ref[:, h * HD : (h + 1) * HD].astype(jnp.float32)
    load_b.wait()

    def put(j, c):
        pltpu.make_async_copy(space.at[pool + place[j]], arrived.at[j], asem).start()
        return c

    lax.fori_loop(0, news, put, 0)
    load_a.wait()
    step = 8

    def body(b, c):
        scores, values = [], []
        for i in range(step):
            r = b * step + i
            at = [table[r * maxp + k] for k in range(maxp)]
            keys = jnp.concatenate([space[a, :, :HD] for a in at], axis=0)
            q = qs[pl.ds(pl.multiple_of(r * 8, 8), 8), :].astype(jnp.bfloat16)
            s = lax.dot_general(
                q, keys, (((1,), (1,)), ((), ())), preferred_element_type=jnp.float32
            ) * (HD ** (-0.5))
            pos = lax.broadcasted_iota(jnp.int32, s.shape, 1)
            scores.append(jnp.where(pos < lens[r], s, NEG))
            values.append(at)
        s = jnp.concatenate(scores, axis=0)
        e = jnp.exp(s - jnp.max(s, axis=1, keepdims=True))
        p = e / jnp.sum(e, axis=1, keepdims=True)
        for i in range(step):
            vals = jnp.concatenate([space[a, :, HD:] for a in values[i]], axis=0)
            o = jnp.dot(
                p[i * 8 : (i + 1) * 8].astype(jnp.bfloat16),
                vals,
                preferred_element_type=jnp.float32,
            )
            att[pl.ds(pl.multiple_of((b * step + i) * 8, 8), 8), :] = o
        return c

    lax.fori_loop(0, reqs // step, body, 0)
    for h in range(heads):
        out_ref[:, h * HD : (h + 1) * HD] = att[pl.ds(h, reqs, stride=8), :].astype(jnp.bfloat16)

    def done(j, c):
        pltpu.make_async_copy(space.at[pool + place[j]], arrived.at[j], asem).wait()
        return c

    lax.fori_loop(0, news, done, 0)


def attend(queries, resident, recv, table, lens, place):
    reqs, width = queries.shape
    pool, page, kvw = resident.shape
    smem = pl.BlockSpec(memory_space=pltpu.SMEM)
    vmem = pl.BlockSpec(memory_space=pltpu.VMEM)
    hbm = pl.BlockSpec(memory_space=pl.ANY)
    return pl.pallas_call(
        functools.partial(attend_kernel, pool),
        out_shape=(
            jax.ShapeDtypeStruct((reqs, width), jnp.bfloat16),
            jax.ShapeDtypeStruct((place.shape[0], page, kvw), jnp.bfloat16),
        ),
        in_specs=[smem, smem, smem, vmem, hbm, hbm],
        out_specs=(vmem, hbm),
        scratch_shapes=[
            pltpu.VMEM((pool + recv.shape[0], page, kvw), jnp.bfloat16),
            pltpu.VMEM((reqs * 8, LANES), jnp.float32),
            pltpu.VMEM((reqs * 8, LANES), jnp.float32),
            pltpu.SemaphoreType.DMA((2,)),
            pltpu.SemaphoreType.DMA,
        ],
        compiler_params=pltpu.CompilerParams(vmem_limit_bytes=40 << 20),
        name="attend",
    )(table, lens, place, queries, resident, recv)


def chain_kernel(
    n, tps, place, held, mix, down, up, out_ref,
    send, got, back, fin, part, parts, ss, rs, sb, rb, st, rt,
):
    reqs, width = mix.shape
    heads = width // HD
    slots, rank = down.shape[0], down.shape[1]
    rows = n * 8
    me, tp = lax.axis_index("req"), lax.axis_index("tp")
    barrier = pltpu.get_barrier_semaphore()

    def hello(d, c):
        pl.semaphore_signal(
            barrier, inc=1, device_id={"req": lax.rem(me + d, n)}, device_id_type=MESH
        )
        return c

    lax.fori_loop(1, n, hello, 0)
    for d in range(1, tps):
        pl.semaphore_signal(
            barrier, inc=1, device_id={"tp": lax.rem(tp + d, tps)}, device_id_type=MESH
        )

    slot_of = lax.broadcasted_iota(jnp.int32, (rows, reqs), 0)
    put = jnp.where(slot_of == place[...], 1.0, 0.0).astype(jnp.bfloat16)
    g = jnp.dot(put, mix[...], preferred_element_type=jnp.float32)
    zero = jnp.zeros((8, LANES), jnp.float32)
    for d in range(n):
        block = [g[d * 8 : (d + 1) * 8, h * HD : (h + 1) * HD] for h in range(heads)]
        block += [zero] * (8 - heads)
        send[d] = jnp.concatenate(block, axis=0).astype(jnp.bfloat16)
    pl.semaphore_wait(barrier, n - 1 + tps - 1)

    def go(src, dst, s_sem, r_sem):
        def start(d, c):
            to = lax.rem(me + d, n)
            pltpu.make_async_remote_copy(
                src_ref=src.at[to], dst_ref=dst.at[me], send_sem=s_sem.at[d], recv_sem=r_sem.at[d],
                device_id={"req": to}, device_id_type=MESH,
            ).start()
            return c

        lax.fori_loop(1, n, start, 0)

    def finish(src, dst, s_sem, r_sem):
        def wait(d, c):
            to = lax.rem(me + d, n)
            frm = lax.rem(me + n - d, n)
            pltpu.make_async_remote_copy(
                src_ref=src.at[to], dst_ref=dst.at[frm], send_sem=s_sem.at[d], recv_sem=r_sem.at[d],
                device_id={"req": to}, device_id_type=MESH,
            ).wait()
            return c

        lax.fori_loop(1, n, wait, 0)

    go(send, got, ss, rs)
    got[me] = send[me]
    finish(send, got, ss, rs)

    x = got[...].astype(jnp.float32)
    a = jnp.concatenate(
        [x[:, h * 8 : (h + 1) * 8, :].reshape(rows, LANES) for h in range(heads)], axis=1
    ).astype(jnp.bfloat16)
    lane = lax.broadcasted_iota(jnp.int32, (rows, LANES), 1)
    per = LANES // rank
    hs = held[...]
    total = jnp.zeros((rows, LANES), jnp.float32)
    for c in range(slots // per):
        w = down[c * per : (c + 1) * per].reshape(per * rank, width)
        s = lax.dot_general(a, w, (((1,), (1,)), ((), ())), preferred_element_type=jnp.float32)
        total = total + jnp.where(hs == c * per + lane // rank, s, 0.0)
    total = total + pltpu.roll(total, rank, 1)
    half = rows // 2
    low = lax.broadcasted_iota(jnp.int32, (half, LANES), 1) < rank
    part[...] = jnp.where(low, total[:half], total[half:])
    copies = []
    for d in range(1, tps):
        copies.append(
            pltpu.make_async_remote_copy(
                src_ref=part, dst_ref=parts.at[d - 1], send_sem=st.at[d - 1], recv_sem=rt.at[d - 1],
                device_id={"tp": lax.rem(tp + d, tps)}, device_id_type=MESH,
            )
        )
        copies[-1].start()
    for copy in copies:
        copy.wait()
    acc = part[...]
    for d in range(tps - 1):
        acc = acc + parts[d]
    turned = pltpu.roll(acc, rank, 1)
    shrunk = jnp.concatenate(
        [jnp.where(low, acc, turned), jnp.where(low, turned, acc)], axis=0
    ).astype(jnp.bfloat16)
    spread = jnp.concatenate(
        [
            jnp.where(hs == c * per + lane // rank, shrunk, jnp.zeros((), jnp.bfloat16))
            for c in range(slots // per)
        ],
        axis=1,
    )
    for h in range(heads):
        w = up[:, :, h * HD : (h + 1) * HD].reshape(slots * rank, HD)
        t = jnp.dot(spread, w, preferred_element_type=jnp.float32) * low_rank_scale
        t = t.astype(jnp.bfloat16).astype(jnp.float32)
        part2 = t.reshape(n, 8, LANES)
        fin[:, h * 8 : (h + 1) * 8, :] = part2
    fin[:, heads * 8 :, :] = jnp.zeros((n, 64 - heads * 8, LANES), jnp.float32)
    send[...] = fin[...].astype(jnp.bfloat16)
    go(send, back, sb, rb)
    back[me] = send[me]
    finish(send, back, sb, rb)
    y = back[...].astype(jnp.float32)
    b = jnp.concatenate(
        [y[:, h * 8 : (h + 1) * 8, :].reshape(rows, LANES) for h in range(heads)], axis=1
    ).astype(jnp.bfloat16)
    out_ref[...] = lax.dot_general(
        put, b, (((0,), (0,)), ((), ())), preferred_element_type=jnp.float32
    ).astype(jnp.bfloat16)


def chain(n, tps, place, held, mixed, down, up):
    reqs, width = mixed.shape
    vmem = pl.BlockSpec(memory_space=pltpu.VMEM)
    dma = pltpu.SemaphoreType.DMA
    rows = n * 8
    return pl.pallas_call(
        functools.partial(chain_kernel, n, tps),
        out_shape=jax.ShapeDtypeStruct((reqs, width), jnp.bfloat16),
        in_specs=[vmem] * 5,
        out_specs=vmem,
        scratch_shapes=[
            pltpu.VMEM((n, 64, LANES), jnp.bfloat16),
            pltpu.VMEM((n, 64, LANES), jnp.bfloat16),
            pltpu.VMEM((n, 64, LANES), jnp.bfloat16),
            pltpu.VMEM((n, 64, LANES), jnp.float32),
            pltpu.VMEM((rows // 2, LANES), jnp.float32),
            pltpu.VMEM((tps - 1, rows // 2, LANES), jnp.float32),
            dma((n,)), dma((n,)), dma((n,)), dma((n,)), dma((tps - 1,)), dma((tps - 1,)),
        ],
        compiler_params=pltpu.CompilerParams(
            collective_id=0, has_side_effects=True, vmem_limit_bytes=40 << 20
        ),
        name="chain",
    )(place, held, mixed, down, up)


def local(
    queries,
    resident_kv,
    swap_kv,
    page_table,
    lengths,
    resume_source,
    resume_page,
    seg_lengths,
    segment_adapter_holder,
    seg_slot,
    adapter_down,
    adapter_up,
):
    devices = lax.axis_size("req")
    tps = lax.axis_size("tp")
    own_index = lax.axis_index("req")
    req_count = queries.shape[0]
    pool = resident_kv.shape[0]
    res_rows = resume_page.shape[0] // devices
    res_cap = max(2, 2 * res_rows // devices)
    res_owner = resume_source[:, 0].reshape(devices, res_rows)
    res_rank = earlier_same(res_owner, devices)
    send_page = pack_table(
        res_owner, res_rank, resume_page.reshape(devices, res_rows), own_index, res_cap
    )
    arriving = lax.all_to_all(swap_kv[send_page], "req", split_axis=0, concat_axis=0, tiled=True)
    my_res_owner = lax.dynamic_index_in_dim(res_owner, own_index, 0, keepdims=False)
    my_res_rank = lax.dynamic_index_in_dim(res_rank, own_index, 0, keepdims=False)
    recv = arriving.reshape((devices * res_cap,) + arriving.shape[2:])
    place_res = my_res_owner * res_cap + my_res_rank
    flat = page_table.reshape(-1)
    where_new = jnp.sum(
        jnp.where(
            flat[:, None] - pool == jnp.arange(res_rows, dtype=jnp.int32)[None, :], place_res[None, :], 0
        ),
        axis=1,
    )
    table = jnp.where(flat < pool, flat, pool + where_new)
    mixed, arrived = attend(queries, resident_kv, recv, table, lengths, place_res)

    segs = seg_lengths.shape[1]
    sizes_row = seg_lengths[0]
    seg_ends = jnp.cumsum(sizes_row)
    seg_starts = seg_ends - sizes_row
    positions = jnp.arange(req_count, dtype=jnp.int32)
    member = jnp.sum((positions[:, None] >= seg_ends[None, :]).astype(jnp.int32), axis=1)
    within = positions - seg_starts[member]
    seg_cap = max(2, 2 * segs // devices)
    owners = segment_adapter_holder[:, 0].reshape(devices, segs)
    owner_rank = earlier_same(owners, devices)
    slots_all = seg_slot.reshape(devices, segs)
    my_owner = lax.dynamic_index_in_dim(owners, own_index, 0, keepdims=False)
    my_rank = lax.dynamic_index_in_dim(owner_rank, own_index, 0, keepdims=False)
    held_slot = pack_table(owners, owner_rank, slots_all, own_index, seg_cap)
    place = ((my_owner * seg_cap + my_rank)[member]) * SEGMAX + within
    row_slot = jnp.repeat(held_slot.reshape(-1), SEGMAX)[:, None]
    adapter_increment = chain(
        devices, tps, place[None, :], row_slot, mixed, adapter_down, adapter_up
    )
    return (mixed, adapter_increment, arrived)


def solution(mesh):
    return jax.shard_map(
        local,
        mesh=mesh,
        in_specs=(
            P("req", "tp"),
            P("req", None, "tp"),
            P("req", None, "tp"),
            P("req", None),
            P("req"),
            P(),
            P(),
            P("req", None),
            P(),
            P(),
            P("req", None, "tp"),
            P("req", None, "tp"),
        ),
        out_specs=(P("req", "tp"), P("req", "tp"), P("req", None, "tp")),
        check_vma=False,
    )
```

time: 482 us -> 176 us (0.37)
  waiting for transfers between devices: 313 us -> 87.8 us
  local copies, waits for them, and re-layouts: 76.8 us -> 11.4 us
  Pallas kernels: 0 us -> 57.4 us
  blocking collectives: 24.7 us -> 0 us
  starting transfers between devices: 35.7 us -> 12.1 us
  matrix products: 14.8 us -> 0 us
  other arithmetic: 13.4 us -> 5.83 us
    all_to_all x2 -> x0, waiting for transfers between devices: 227 us -> none  [the longest x1 160 us: local(): lax.all_to_all(adapter_down[send_slot], 'req', split_axis=0, concat_axis=...]
    pallas_call x0 -> x2, Pallas kernels: none -> 57.4 us  [the longest x1 48.4 us: chain(): pl.pallas_call(functools.partial(chain_kernel, n, tps), out_shape=jax.Sha...]
    gather x9 -> x1, local copies, waits for them, and re-layouts: 38.9 us -> 0.78 us  [local(): place = (my_owner * seg_cap + my_rank)[member] * SEGMAX + within]
    psum x1 -> x0, blocking collectives: 24.7 us -> none  [local(): down_projected = lax.psum(partial_sums, 'tp').astype(jnp.bfloat16)]
    all_to_all x2 -> x0, starting transfers between devices: 23.6 us -> none  [the longest x1 15 us: local(): lax.all_to_all(adapter_up[send_slot], 'req', split_axis=0, concat_axis=0,...]
    slice x1 -> x0, local copies, waits for them, and re-layouts: 17.5 us -> none  [attend(): picked[:, :, :, 0, :]]
    reshape x2, local copies, waits for them, and re-layouts: 12.6 us -> 0.22 us  [the longest x1 0.11 us: local(): row_slot = jnp.repeat(held_slot.reshape(-1), SEGMAX)[:, None]]
    dot_general x3 -> x0, matrix products: 10.1 us -> none  [the longest x1 4.12 us: attend(): jnp.einsum('rkgt,rtkd->rkgd', probabilities, picked[:, :, :, 1, :], prefe...]
  transfers between devices with their start and end apart: 3 -> 1, of which waited for: 3 -> 1; matrix products, arithmetic and copies ran while one was open for 18% -> 3% of each run, Pallas kernels for 0% -> 0%
where the time goes in v2:
time: 176 us; the launch traced here: 175 us
  waiting for transfers between devices  87.8 us (50%)
  Pallas kernels  57.4 us (33%)
  starting transfers between devices  12.1 us (7%)
  local copies, waits for them, and re-layouts  11.4 us (6%)
  other arithmetic  5.83 us (3%)
    all_to_all x1, waiting for transfers between devices, local(): lax.all_to_all(swap_kv[send_page], 'req', split_axis=0, concat_axis=0, ti...  87.8 us
    pallas_call x1, Pallas kernels, chain(): pl.pallas_call(functools.partial(chain_kernel, n, tps), out_shape=jax.Sha...  48.4 us
    all_to_all x1, starting transfers between devices, local(): lax.all_to_all(swap_kv[send_page], 'req', split_axis=0, concat_axis=0, ti...  12.1 us
    pallas_call x1, Pallas kernels, attend(): pl.pallas_call(functools.partial(attend_kernel, pool), out_shape=(jax.Sha...  8.97 us
    unnamed x25, local copies, waits for them, and re-layouts  4.98 us
  transfers between devices with their start and end apart: 1, of which 1 were waited for; matrix products, arithmetic and copies ran while one was open for 3% of the time, Pallas kernels for 0%

profile of v2, /device:TPU:1, one launch (start us, length us, event | category | flops | bytes accessed | tf_op | source)
XLA Modules:
  0.0 175.4 jit_solution(12587941848632669455)
XLA Ops:
  0.6 0.0 copy-start
  0.6 0.5 broadcast.115
  1.2 1.4 reduce.11
  2.5 0.1 reshape_squeeze.6
  2.6 0.1 copy.44
  2.7 1.7 select_reduce_fusion
  4.4 0.1 copy.46
  4.5 0.8 broadcast_in_dim.64
  5.3 0.1 select_reduce_fusion.1
  5.4 0.1 copy.47
  5.5 0.1 reshape.124
  5.6 0.0 copy-done
  5.6 2.8 %gather_fusion = bf16[128,64,256]{2,1,0:T(8,128)(2,1)} fusion(bf16[32,64,256]{2,1,0:T(8,128)(2,1)S(1)} %copy-done, s32[1024]{0:T(1024)S(1)} %pad_clamp_fusion.1), kind=kCustom, calls=%fused_computation | custom fusion | bytes 8389120 | tf_op jit(solution)/shard_map/gather | solution.py:295
  8.4 0.0 copy-start.9
  8.4 0.0 copy-start.8
  8.4 0.0 copy-start.10
  8.4 0.0 copy-start.7
  8.4 0.0 copy-start.4
  8.5 0.0 copy-start.6
  8.5 12.1 %all-to-all-start = ((bf16[32,4,64,256]{3,2,1,0:T(8,128)(2,1)}), bf16[32,4,64,256]{3,2,1,0:T(8,128)(2,1)}, u32[]{:S(2)}, u32[]{:S(2)}) async-start(bf16[32,4,64,256]{3,2,1,0:T(8,128)(2,1)} %bitcast.21), calls=%async_computation | async-start | bytes 8388608 | tf_op jit(solution)/shard_map/all_to_all | solution.py:295
  20.6 0.0 copy-done.9
  20.6 0.1 copy.43
  20.7 0.1 reshape.117
  20.8 0.0 copy-done.8
  20.8 0.7 reduce.12
  21.5 0.1 reshape_squeeze.7
  21.6 0.1 copy.48
  21.7 0.0 copy-done.10
  21.7 0.1 copy.50
  21.7 0.1 reduce-window.8
  21.8 0.1 reduce.4
  21.9 1.0 fusion.12
  23.0 0.1 copy.51
  23.0 0.2 add_reduce_fusion.1
  23.2 0.1 convert_reduce_fusion
  23.3 0.8 gather_fusion.1
  24.1 0.8 gather_fusion.2
  24.9 0.0 copy-done.7
  24.9 0.1 broadcast_in_dim.67
  25.0 0.1 select_reduce_fusion.3
  25.1 0.1 copy.52
  25.2 0.1 reshape.121
  25.3 0.1 broadcast_in_dim.70
  25.4 0.1 broadcast_in_dim_reshape.3.held
  25.5 0.2 add_reduce_fusion.place
  25.7 0.1 select_reduce_fusion.2
  25.8 87.8 %all-to-all-done = bf16[32,4,64,256]{3,2,1,0:T(8,128)(2,1)} async-done(((bf16[32,4,64,256]{3,2,1,0:T(8,128)(2,1)}), bf16[32,4,64,256]{3,2,1,0:T(8,128)(2,1)}, u32[]{:S(2)}, u32[]{:S(2)}) %all-to-all-start) | async-done | bytes 4194336 | tf_op jit(solution)/shard_map/all_to_all | solution.py:295
  113.6 0.0 copy-done.4
  113.6 0.0 copy-done.6
  113.7 0.0 copy-start.1
  113.7 2.8 %copy-done.1 = bf16[192,64,256]{2,1,0:T(8,128)(2,1)S(1)} copy-done((bf16[192,64,256]{2,1,0:T(8,128)(2,1)S(1)}, bf16[192,64,256]{2,1,0:T(8,128)(2,1)}, u32[]{:S(2)}) %copy-start.1) | copy-done | bytes 6291480
  116.4 0.0 copy-start.2
  116.4 0.0 copy-start.3
  116.4 9.0 %attend.1 = (bf16[64,896]{1,0:T(8,128)(2,1)}, bf16[64,64,256]{2,1,0:T(8,128)(2,1)}) custom-call(s32[256]{0:T(256)S(1)} %compare_select_fusion.1.table, s32[64]{0:T(128)S(1)} %copy-done.6, s32[64]{0:T(128)S(1)} %add_reduce_fusion.place, bf16[64,896]{1,0:T(8,128)(2,1)S(1)} %copy-done.4, bf16[192,64,256]{2,1,0:T(8,128)(2,1)S(1)} %copy-done.1, ...), custom_call_target="tpu_custom_call" | custom-call | tf_op jit(solution)/shard_map/attend/pallas_call | solution.py:102
  125.4 0.0 copy-done.2
  125.4 0.0 copy-done.3
  125.4 0.0 copy-start.5
  125.5 0.9 copy-done.5
  126.3 48.4 %chain.1 = bf16[64,896]{1,0:T(8,128)(2,1)S(1)} custom-call(s32[1,64]{1,0:T(1,128)S(1)} %fusion.11.place, s32[256,1]{1,0:T(8,128)S(1)} %broadcast_in_dim_reshape.3.held, bf16[64,896]{1,0:T(8,128)(2,1)S(1)} %copy-done.5, bf16[16,64,896]{2,1,0:T(8,128)(2,1)S(1)} %copy-done.2, bf16[16,64,896]{2,1,0:T(8,128)(2,1)S(1)} %copy-done.3), custom_call_target="tpu_custom_call" | custom-call | tf_op jit(solution)/shard_map/chain/pallas_call | solution.py:248
  174.8 0.6 copy.55
  (10 shorter events, 0.1 us)
Async XLA Ops:
  0.6 5.0 %copy-start = (bf16[32,64,256]{2,1,0:T(8,128)(2,1)S(1)}, bf16[32,64,256]{2,1,0:T(8,128)(2,1)}, u32[]{:S(2)}) copy-start(bf16[32,64,256]{2,1,0:T(8,128)(2,1)} %param.14) | copy-start | bytes 3145732
  8.4 12.2 %copy-start.9 = (s32[64,4]{0,1:T(4,128)S(1)}, s32[64,4]{0,1:T(4,128)}, u32[]{:S(2)}) copy-start(s32[64,4]{0,1:T(4,128)} %param.15) | copy-start | bytes 3076
  8.4 12.4 %copy-start.8 = (s32[1024,1]{0,1:T(1,128)S(1)}, s32[1024,1]{0,1:T(1,128)}, u32[]{:S(2)}) copy-start(s32[1024,1]{0,1:T(1,128)} %param.20) | copy-start | bytes 12292
  8.4 13.2 %copy-start.10 = (s32[1,32]{1,0:T(1,128)S(1)}, s32[1,32]{1,0:T(1,128)}, u32[]{:S(2)}) copy-start(s32[1,32]{1,0:T(1,128)} %param.19) | copy-start | bytes 388
  8.4 16.5 %copy-start.7 = (s32[1024]{0:T(1024)S(1)}, s32[1024]{0:T(1024)}, u32[]{:S(2)}) copy-start(s32[1024]{0:T(1024)} %param.21) | copy-start | bytes 12292
  8.4 105.2 %copy-start.4 = (bf16[64,896]{1,0:T(8,128)(2,1)S(1)}, bf16[64,896]{1,0:T(8,128)(2,1)}, u32[]{:S(2)}) copy-start(bf16[64,896]{1,0:T(8,128)(2,1)} %q_ref.1) | copy-start | bytes 344068
  8.5 105.2 %copy-start.6 = (s32[64]{0:T(128)S(1)}, s32[64]{0:T(128)}, u32[]{:S(2)}) copy-start(s32[64]{0:T(128)} %lens.1) | copy-start | bytes 772
  8.5 105.2 %all-to-all-start = ((bf16[32,4,64,256]{3,2,1,0:T(8,128)(2,1)}), bf16[32,4,64,256]{3,2,1,0:T(8,128)(2,1)}, u32[]{:S(2)}, u32[]{:S(2)}) async-start(bf16[32,4,64,256]{3,2,1,0:T(8,128)(2,1)} %bitcast.21), calls=%async_computation | async-start | bytes 8388608 | tf_op jit(solution)/shard_map/all_to_all | solution.py:295
  113.7 2.8 %copy-start.1 = (bf16[192,64,256]{2,1,0:T(8,128)(2,1)S(1)}, bf16[192,64,256]{2,1,0:T(8,128)(2,1)}, u32[]{:S(2)}) copy-start(bf16[192,64,256]{2,1,0:T(8,128)(2,1)} %resident.1) | copy-start | bytes 18874372
  116.4 9.0 %copy-start.2 = (bf16[16,64,896]{2,1,0:T(8,128)(2,1)S(1)}, bf16[16,64,896]{2,1,0:T(8,128)(2,1)}, u32[]{:S(2)}) copy-start(bf16[16,64,896]{2,1,0:T(8,128)(2,1)} %down.1) | copy-start | bytes 5505028
  116.4 9.0 %copy-start.3 = (bf16[16,64,896]{2,1,0:T(8,128)(2,1)S(1)}, bf16[16,64,896]{2,1,0:T(8,128)(2,1)}, u32[]{:S(2)}) copy-start(bf16[16,64,896]{2,1,0:T(8,128)(2,1)} %up.1) | copy-start | bytes 5505028
  125.4 0.9 copy-start.5

commit v3 on v2

v3 whole, which is shorter than its diff:
```python
import functools

import jax
import jax.numpy as jnp
from jax import lax
from jax.experimental import pallas as pl
from jax.experimental.pallas import tpu as pltpu
from jax.sharding import PartitionSpec as P

HD = 128
SEGMAX = 4
LANES = 128
MESH = pl.DeviceIdType.MESH
NEG = -1e30
RZ, RX = 8, 4
CAP = 4
CHUNK = 8
NEAR = 24
FAR = 8

low_rank_scale = 2.0


def iota(shape, dim):
    return lax.broadcasted_iota(jnp.int32, shape, dim)


def ones(mask):
    return jnp.where(mask, 1.0, 0.0)


def mm(a, b):
    return jnp.dot(
        a.astype(jnp.bfloat16), b.astype(jnp.bfloat16), preferred_element_type=jnp.float32
    )


def mmt(a, b):
    return lax.dot_general(
        a.astype(jnp.bfloat16),
        b.astype(jnp.bfloat16),
        (((1,), (1,)), ((), ())),
        preferred_element_type=jnp.float32,
    )


def before(n, block):
    r, c = iota((n, n), 0), iota((n, n), 1)
    return ones((r < c) & (r // block == c // block))


def row_of(x, i):
    return jnp.sum(jnp.where(iota(x.shape, 0) == i, x, jnp.zeros((), x.dtype)), axis=0, keepdims=True)


def ring_plan(source, wanted, zi, xi, stores, pages, per_block):
    shape = (RZ, pages)
    zs = iota(shape, 0)
    need = []
    for zd in range(RZ):
        total = jnp.zeros(shape, jnp.float32)
        for h in range(2):
            s = source[2 * zd + h : 2 * zd + h + 1]
            w = wanted[2 * zd + h : 2 * zd + h + 1]
            a = ones(iota((RZ, LANES), 0) * RX + xi == s)
            b = ones(iota((pages, LANES), 0) == w)
            total = total + mmt(a, b)
        need.append(total)
    at = {}
    for k in (3, 4, 5):
        at[k] = jnp.zeros(shape, jnp.float32)
        for zd in range(RZ):
            at[k] = jnp.where(lax.rem(zd - zs + RZ, RZ) == k, need[zd], at[k])
        at[k] = ones(at[k] > 0.5)
    tri = before(pages, pages)
    far = at[4]
    far_up = far * ones(mm(far, tri) < FAR - 0.5)
    far_down = far - far_up
    lists = {}
    for name, f4, f3 in (("up", far_up, at[3]), ("down", far_down, at[5])):
        f3 = f3 * (1.0 - f4)
        place4 = mm(f4, tri)
        place3 = jnp.sum(f4, axis=1, keepdims=True) + mm(f3, tri)
        lists[name] = (f4, f3, place4, f4 * place4 + f3 * place3)
    page_id = iota(shape, 1).astype(jnp.float32)
    k = lax.rem(zi - zs + RZ, RZ)
    spot4 = jnp.where(far_up > 0.5, lists["up"][2], FAR + lists["down"][2])
    spot = jnp.where(
        k == 3, lists["up"][3], jnp.where(k == 5, lists["down"][3], jnp.where(k == 4, spot4, page_id))
    )
    send = []
    for name, owner in (("up", lax.rem(zi + RZ - 2, RZ)), ("down", lax.rem(zi + 2, RZ))):
        f4, f3, _, place = lists[name]
        used = row_of(f4 + f3, owner)
        p = row_of(place, owner)
        hit = (iota((pages, pages), 0).astype(jnp.float32) == p) & (used > 0.5)
        send.append(
            jnp.sum(
                jnp.where(hit, iota((pages, pages), 1).astype(jnp.float32), 0.0), axis=1, keepdims=True
            )
        )
    tri2 = before(LANES, per_block)
    table = jnp.zeros((RZ, LANES), jnp.float32)
    landing = []
    lane = iota((1, LANES), 1)
    for h in range(2):
        s = row_of(source, 2 * zi + h)
        w = row_of(wanted, 2 * zi + h)
        hot = ones(iota((stores, LANES), 0) == s)
        rank = jnp.sum(hot * mm(hot, tri2), axis=0, keepdims=True)
        landing.append(s.astype(jnp.float32) * CAP + rank)
        v = mm(spot, ones(iota((pages, LANES), 0) == w))
        v = v * ones(iota((RZ, LANES), 0) * RX + xi == s)
        column = (2 * h + lane // per_block) * CAP + rank.astype(jnp.int32)
        table = table + mmt(v, ones(iota((LANES, LANES), 0) == column))
    top = jnp.concatenate(
        [table, landing[0], landing[1], jnp.zeros((RZ - 2, LANES), jnp.float32)], axis=0
    )
    wide = iota((pages, LANES), 1)
    tail = jnp.where(wide == 0, send[0], jnp.where(wide == 1, send[1], 0.0))
    return jnp.concatenate([top, tail], axis=0).astype(jnp.int32)


def chain_plan(n, reqs, sizes, holder, slot, me):
    segs = sizes.shape[1]
    rows = n * 8
    blocks = LANES // segs
    tri = before(LANES, segs)
    mine = ones(holder == me)
    order = mm(mine, tri)
    spread = iota((rows, holder.shape[0]), 0) // (8 * blocks) == iota((rows, holder.shape[0]), 1)
    y = []
    for q in range(2):
        x = jnp.where((mine > 0.5) & (jnp.abs(order - q) < 0.5), slot, 0).astype(jnp.float32)
        y.append(mm(ones(spread), x))
    number = iota((rows, LANES), 0)
    pick = jnp.where(lax.rem(number // 4, 2) == 0, y[0], y[1])
    pick = jnp.where(iota((rows, LANES), 1) // segs == lax.rem(number // 8, blocks), pick, 0.0)
    held = jnp.sum(pick, axis=1, keepdims=True).astype(jnp.int32)

    own = row_of(holder, me // blocks)
    hot = ones(iota((n, LANES), 0) == own)
    rank = jnp.sum(hot * mm(hot, tri), axis=0, keepdims=True)
    value = (own.astype(jnp.float32) * 2 + rank) * SEGMAX
    diag = iota((segs, LANES), 1) == lax.rem(me, blocks) * segs + iota((segs, LANES), 0)
    value = jnp.sum(jnp.where(diag, value, 0.0), axis=1, keepdims=True)
    size = sizes.astype(jnp.float32)
    square = iota((segs, segs), 1) == iota((segs, segs), 0)
    wide = jnp.where(square, size, 0.0)
    size = jnp.sum(wide, axis=1, keepdims=True)
    start = jnp.sum(
        jnp.where(
            iota((segs, segs), 1) < iota((segs, segs), 0), sizes.astype(jnp.float32), 0.0
        ),
        axis=1,
        keepdims=True,
    )
    r = iota((segs, reqs), 1).astype(jnp.float32)
    inside = (r >= start) & (r < start + size)
    place = jnp.sum(jnp.where(inside, value - start + r, 0.0), axis=0, keepdims=True)
    return place.astype(jnp.int32), held


def by_heads(x, rows, heads):
    return jnp.concatenate(
        [x[:, h * 8 : (h + 1) * 8, :].reshape(rows, LANES) for h in range(heads)], axis=1
    )


def main_kernel(
    n, tps,
    table, lens, q_ref, source, wanted, sizes, holder, slot, resident, swap, down_in, up_in,
    out_ref, delta_ref, arrived,
    space, store, near_up, near_down, next_up, next_down, on_up, on_down, third_up, third_down,
    fourth, crossing, arr, qs, att, down, up, send, got, back, fin, part, parts, plan, book,
    load, s1, r1, s2, r2, s3, r3, s4, r4, sx, rx, ss, rs, sb, rb, st, rt,
):
    reqs, width = q_ref.shape
    heads = width // HD
    pool, page = resident.shape[0], resident.shape[1]
    maxp = table.shape[1]
    news = arr.shape[0]
    pages = store.shape[0]
    slots, rank = down.shape[0], down.shape[1]
    rows = n * 8
    me, tp = lax.axis_index("req"), lax.axis_index("tp")
    zi, xi = me // RX, lax.rem(me, RX)
    above = lax.rem(zi + 1, RZ) * RX + xi
    below = lax.rem(zi + RZ - 1, RZ) * RX + xi
    barrier = pltpu.get_barrier_semaphore()

    loads = [
        pltpu.make_async_copy(swap, store, load.at[0]),
        pltpu.make_async_copy(resident, space.at[pl.ds(0, pool)], load.at[1]),
        pltpu.make_async_copy(down_in, down, load.at[2]),
        pltpu.make_async_copy(up_in, up, load.at[3]),
    ]
    loads[0].start()

    def hello(d, c):
        pl.semaphore_signal(
            barrier, inc=1, device_id={"req": lax.rem(me + d, n)}, device_id_type=MESH
        )
        return c

    lax.fori_loop(1, n, hello, 0)
    for d in range(1, tps):
        pl.semaphore_signal(
            barrier, inc=1, device_id={"tp": lax.rem(tp + d, tps)}, device_id_type=MESH
        )
    loads[0].wait()
    pl.semaphore_wait(barrier, n - 1 + tps - 1)

    def hop(src, dst, ssem, rsem, to):
        return pltpu.make_async_remote_copy(
            src_ref=src, dst_ref=dst, send_sem=ssem, recv_sem=rsem,
            device_id={"req": to}, device_id_type=MESH,
        )

    sides = (above, below)
    near, nxt, on, third = (
        (near_up, near_down), (next_up, next_down), (on_up, on_down), (third_up, third_down)
    )

    def part_of(ref, c):
        return ref.at[pl.ds(c * CHUNK, CHUNK)]

    first, second, later, last = [], [], [], []
    for c in range(pages // CHUNK):
        for w in range(2):
            first.append(
                hop(part_of(store, c), part_of(near[w], c), s1.at[w, c], r1.at[w, c], sides[w])
            )
            second.append(
                hop(part_of(near[w], c), part_of(nxt[w], c), s2.at[w, c], r2.at[w, c], sides[w])
            )
    for c in range(NEAR // CHUNK):
        for w in range(2):
            later.append(
                hop(part_of(on[w], c), part_of(third[w], c), s3.at[w, c], r3.at[w, c], sides[w])
            )
    for w in range(2):
        last.append(
            hop(third[w].at[pl.ds(0, FAR)], part_of(fourth, w), s4.at[w], r4.at[w], sides[w])
        )
    for copy in first:
        copy.start()
    for copy in loads[1:]:
        copy.start()

    plan[...] = ring_plan(source[...], wanted[...], zi, xi, n, pages, news)
    enter = pltpu.make_async_copy(plan, book, load.at[0])
    enter.start()
    slot_place, hs = chain_plan(n, reqs, sizes[...], holder[...], slot[...], me)
    put = ones(iota((rows, reqs), 0) == slot_place).astype(jnp.bfloat16)
    qs[...] = jnp.zeros_like(qs)
    for h in range(heads):
        qs[pl.ds(h, reqs, stride=8), :] = q_ref[:, h * HD : (h + 1) * HD].astype(jnp.float32)
    enter.wait()

    def within(i, ref):
        return jnp.clip(i, 0, ref.shape[0] - 1)

    def land(z, x):
        return pool + (z * RX + x) * CAP

    def cross_copy(k, dx):
        z = lax.rem(zi + RZ - k, RZ)
        return hop(
            crossing.at[k, dx - 1], space.at[pl.ds(land(z, xi), CAP)],
            sx.at[k, dx - 1], rx.at[k, dx - 1], z_row(dx),
        )

    def z_row(dx):
        return zi * RX + lax.rem(xi + dx, RX)

    def cross(k, ref):
        z = lax.rem(zi + RZ - k, RZ)
        for dx in (2, 1, 3):
            xd = lax.rem(xi + dx, RX)
            for r in range(CAP):
                crossing[k, dx - 1, r] = ref[within(book[z, xd * CAP + r], ref)]
            cross_copy(k, dx).start()
        for r in range(CAP):
            space[land(z, xi) + r] = ref[within(book[z, xi * CAP + r], ref)]

    cross(0, store)
    for a, b in zip(first, second):
        a.wait_recv()
        b.start()
    cross(1, near_up)
    cross(7, near_down)
    for copy in second:
        copy.wait_recv()
    for w in range(2):
        for c in range(NEAR // CHUNK):
            for i in range(CHUNK):
                on[w][c * CHUNK + i] = nxt[w][within(book[16 + c * CHUNK + i, w], nxt[w])]
            later[c * 2 + w].start()
    cross(2, next_up)
    cross(6, next_down)
    for i, copy in enumerate(later):
        copy.wait_recv()
        if i < 2:
            last[i].start()
    cross(3, third_up)
    cross(5, third_down)
    for copy in last:
        copy.wait_recv()
    cross(4, fourth)
    for copy in loads[1:]:
        copy.wait()
    for copy in first + second + later + last:
        copy.wait_send()
    for k in range(RZ):
        for dx in range(1, RX):
            cross_copy(k, dx).wait_send()
            z = lax.rem(zi + RZ - k, RZ)
            x = lax.rem(xi + RX - dx, RX)
            hop(
                crossing.at[k, dx - 1], space.at[pl.ds(land(z, x), CAP)],
                sx.at[k, dx - 1], rx.at[k, dx - 1], z_row(dx),
            ).wait_recv()

    def spot(j):
        return pool + jnp.clip(book[8 + xi // 2, lax.rem(xi, 2) * news + j], 0, n * CAP - 1)

    def pick(j, c):
        arr[j] = space[spot(j)]
        return c

    lax.fori_loop(0, news, pick, 0)
    keep = pltpu.make_async_copy(arr, arrived, load.at[0])
    keep.start()

    step = 8

    def page_at(r, k):
        t = table[r, k]
        return jnp.where(t < pool, jnp.clip(t, 0, pool - 1), spot(jnp.clip(t - pool, 0, news - 1)))

    def body(b, c):
        scores, spots = [], []
        for i in range(step):
            r = b * step + i
            at = [page_at(r, k) for k in range(maxp)]
            keys = jnp.concatenate([space[a, :, :HD] for a in at], axis=0)
            q = qs[pl.ds(pl.multiple_of(r * 8, 8), 8), :].astype(jnp.bfloat16)
            s = lax.dot_general(
                q, keys, (((1,), (1,)), ((), ())), preferred_element_type=jnp.float32
            ) * (HD ** (-0.5))
            pos = lax.broadcasted_iota(jnp.int32, s.shape, 1)
            scores.append(jnp.where(pos < lens[r], s, NEG))
            spots.append(at)
        s = jnp.concatenate(scores, axis=0)
        e = jnp.exp(s - jnp.max(s, axis=1, keepdims=True))
        p = e / jnp.sum(e, axis=1, keepdims=True)
        for i in range(step):
            vals = jnp.concatenate([space[a, :, HD:] for a in spots[i]], axis=0)
            o = jnp.dot(
                p[i * 8 : (i + 1) * 8].astype(jnp.bfloat16),
                vals,
                preferred_element_type=jnp.float32,
            )
            att[pl.ds(pl.multiple_of((b * step + i) * 8, 8), 8), :] = o
        return c

    lax.fori_loop(0, reqs // step, body, 0)
    for h in range(heads):
        out_ref[:, h * HD : (h + 1) * HD] = att[pl.ds(h, reqs, stride=8), :].astype(jnp.bfloat16)

    g = jnp.dot(put, out_ref[...], preferred_element_type=jnp.float32)
    zero = jnp.zeros((8, LANES), jnp.float32)

    def go(src, dst, s_sem, r_sem):
        def start(d, c):
            to = lax.rem(me + d, n)
            pltpu.make_async_remote_copy(
                src_ref=src.at[to], dst_ref=dst.at[me], send_sem=s_sem.at[d], recv_sem=r_sem.at[d],
                device_id={"req": to}, device_id_type=MESH,
            ).start()
            return c

        lax.fori_loop(1, n, start, 0)

    def finish(src, dst, s_sem, r_sem):
        def wait(d, c):
            to = lax.rem(me + d, n)
            frm = lax.rem(me + n - d, n)
            pltpu.make_async_remote_copy(
                src_ref=src.at[to], dst_ref=dst.at[frm], send_sem=s_sem.at[d], recv_sem=r_sem.at[d],
                device_id={"req": to}, device_id_type=MESH,
            ).wait()
            return c

        lax.fori_loop(1, n, wait, 0)

    for d in range(n):
        block = [g[d * 8 : (d + 1) * 8, h * HD : (h + 1) * HD] for h in range(heads)]
        block += [zero] * (8 - heads)
        send[d] = jnp.concatenate(block, axis=0).astype(jnp.bfloat16)
    go(send, got, ss, rs)
    got[me] = send[me]
    finish(send, got, ss, rs)

    a = by_heads(got[...].astype(jnp.float32), rows, heads).astype(jnp.bfloat16)
    lane = lax.broadcasted_iota(jnp.int32, (rows, LANES), 1)
    per = LANES // rank
    total = jnp.zeros((rows, LANES), jnp.float32)
    for c in range(slots // per):
        w = down[c * per : (c + 1) * per].reshape(per * rank, width)
        s = lax.dot_general(a, w, (((1,), (1,)), ((), ())), preferred_element_type=jnp.float32)
        total = total + jnp.where(hs == c * per + lane // rank, s, 0.0)
    total = total + pltpu.roll(total, rank, 1)
    half = rows // 2
    low = lax.broadcasted_iota(jnp.int32, (half, LANES), 1) < rank
    part[...] = jnp.where(low, total[:half], total[half:])
    copies = []
    for d in range(1, tps):
        copies.append(
            pltpu.make_async_remote_copy(
                src_ref=part, dst_ref=parts.at[d - 1], send_sem=st.at[d - 1], recv_sem=rt.at[d - 1],
                device_id={"tp": lax.rem(tp + d, tps)}, device_id_type=MESH,
            )
        )
        copies[-1].start()
    for copy in copies:
        copy.wait()
    acc = part[...]
    for d in range(tps - 1):
        acc = acc + parts[d]
    turned = pltpu.roll(acc, rank, 1)
    shrunk = jnp.concatenate(
        [jnp.where(low, acc, turned), jnp.where(low, turned, acc)], axis=0
    ).astype(jnp.bfloat16)
    spread = jnp.concatenate(
        [
            jnp.where(hs == c * per + lane // rank, shrunk, jnp.zeros((), jnp.bfloat16))
            for c in range(slots // per)
        ],
        axis=1,
    )
    for h in range(heads):
        w = up[:, :, h * HD : (h + 1) * HD].reshape(slots * rank, HD)
        t = jnp.dot(spread, w, preferred_element_type=jnp.float32) * low_rank_scale
        fin[:, h * 8 : (h + 1) * 8, :] = t.reshape(n, 8, LANES)
    fin[:, heads * 8 :, :] = jnp.zeros((n, 64 - heads * 8, LANES), jnp.float32)
    send[...] = fin[...].astype(jnp.bfloat16)
    go(send, back, sb, rb)
    back[me] = send[me]
    finish(send, back, sb, rb)
    b = by_heads(back[...].astype(jnp.float32), rows, heads).astype(jnp.bfloat16)
    delta_ref[...] = lax.dot_general(
        put, b, (((0,), (0,)), ((), ())), preferred_element_type=jnp.float32
    ).astype(jnp.bfloat16)
    keep.wait()


def serve(n, tps, table, lens, queries, source, wanted, sizes, holder, slot, resident, swap, down, up):
    reqs, width = queries.shape
    pool, page, kvw = resident.shape
    news = source.size // n
    rows = n * 8
    smem = pl.BlockSpec(memory_space=pltpu.SMEM)
    vmem = pl.BlockSpec(memory_space=pltpu.VMEM)
    hbm = pl.BlockSpec(memory_space=pl.ANY)
    dma = pltpu.SemaphoreType.DMA
    bf16, f32 = jnp.bfloat16, jnp.float32
    stores = swap.shape[0]

    def held(count):
        return pltpu.VMEM((count, page, kvw), bf16)

    return pl.pallas_call(
        functools.partial(main_kernel, n, tps),
        out_shape=(
            jax.ShapeDtypeStruct((reqs, width), bf16),
            jax.ShapeDtypeStruct((reqs, width), bf16),
            jax.ShapeDtypeStruct((news, page, kvw), bf16),
        ),
        in_specs=[smem] * 2 + [vmem] * 6 + [hbm] * 4,
        out_specs=(vmem, vmem, hbm),
        scratch_shapes=[
            held(pool + n * CAP),
            held(stores), held(stores), held(stores), held(stores), held(stores),
            held(NEAR), held(NEAR), held(NEAR), held(NEAR), held(2 * FAR),
            pltpu.VMEM((RZ, RX - 1, CAP, page, kvw), bf16),
            held(news),
            pltpu.VMEM((reqs * 8, LANES), f32),
            pltpu.VMEM((reqs * 8, LANES), f32),
            pltpu.VMEM(down.shape, bf16),
            pltpu.VMEM(up.shape, bf16),
            pltpu.VMEM((n, 64, LANES), bf16),
            pltpu.VMEM((n, 64, LANES), bf16),
            pltpu.VMEM((n, 64, LANES), bf16),
            pltpu.VMEM((n, 64, LANES), f32),
            pltpu.VMEM((rows // 2, LANES), f32),
            pltpu.VMEM((tps - 1, rows // 2, LANES), f32),
            pltpu.VMEM((16 + stores, LANES), jnp.int32),
            pltpu.SMEM((16 + stores, LANES), jnp.int32),
            dma((4,)),
            dma((2, stores // CHUNK)), dma((2, stores // CHUNK)),
            dma((2, stores // CHUNK)), dma((2, stores // CHUNK)),
            dma((2, NEAR // CHUNK)), dma((2, NEAR // CHUNK)), dma((2,)), dma((2,)),
            dma((RZ, RX - 1)), dma((RZ, RX - 1)),
            dma((n,)), dma((n,)), dma((n,)), dma((n,)),
            dma((tps - 1,)), dma((tps - 1,)),
        ],
        compiler_params=pltpu.CompilerParams(
            collective_id=0, has_side_effects=True, vmem_limit_bytes=56 << 20
        ),
        name="serve",
    )(table, lens, queries, source, wanted, sizes, holder, slot, resident, swap, down, up)


def local(
    queries,
    resident_kv,
    swap_kv,
    page_table,
    lengths,
    resume_source,
    resume_page,
    seg_lengths,
    segment_adapter_holder,
    seg_slot,
    adapter_down,
    adapter_up,
):
    return serve(
        lax.axis_size("req"),
        lax.axis_size("tp"),
        page_table,
        lengths,
        queries,
        resume_source.reshape(-1, LANES),
        resume_page.reshape(-1, LANES),
        seg_lengths,
        segment_adapter_holder.reshape(-1, LANES),
        seg_slot.reshape(-1, LANES),
        resident_kv,
        swap_kv,
        adapter_down,
        adapter_up,
    )


def solution(mesh):
    return jax.shard_map(
        local,
        mesh=mesh,
        in_specs=(
            P("req", "tp"),
            P("req", None, "tp"),
            P("req", None, "tp"),
            P("req", None),
            P("req"),
            P(),
            P(),
            P("req", None),
            P(),
            P(),
            P("req", None, "tp"),
            P("req", None, "tp"),
        ),
        out_specs=(P("req", "tp"), P("req", "tp"), P("req", None, "tp")),
        check_vma=False,
    )
```

time: 176 us -> 149 us (0.85)
  waiting for transfers between devices: 87.8 us -> 0 us
  Pallas kernels: 57.4 us -> 141 us
  starting transfers between devices: 12.1 us -> 0 us
  other arithmetic: 5.83 us -> 0 us
  local copies, waits for them, and re-layouts: 11.4 us -> 7.65 us
    all_to_all x1 -> x0, waiting for transfers between devices: 87.8 us -> none  [local(): lax.all_to_all(swap_kv[send_page], 'req', split_axis=0, concat_axis=0, ti...]
    pallas_call x2 -> x1, Pallas kernels: 57.4 us -> 141 us  [serve(): pl.pallas_call(functools.partial(main_kernel, n, tps), out_shape=(jax.Sha...]
    all_to_all x1 -> x0, starting transfers between devices: 12.1 us -> none  [local(): lax.all_to_all(swap_kv[send_page], 'req', split_axis=0, concat_axis=0, ti...]
    gather x3 -> x0, local copies, waits for them, and re-layouts: 4.34 us -> none  [the longest x1 2.79 us: local(): swap_kv[send_page]]
    another operation x4 -> x0, other arithmetic: 2.94 us -> none  [the longest x2 2.77 us: earlier_same(): before = jnp.cumsum(marks, axis=1) - marks]
    unnamed x25 -> x4, local copies, waits for them, and re-layouts: 4.98 us -> 7.65 us
    unnamed x2 -> x0, other arithmetic: 2.03 us -> none
  transfers between devices with their start and end apart: 1 -> 0, of which waited for: 1 -> 0; matrix products, arithmetic and copies ran while one was open for 3% -> 0% of each run, Pallas kernels for 0% -> 0%
where the time goes in v3:
time: 149 us
  Pallas kernels  141 us (95%)
  local copies, waits for them, and re-layouts  7.65 us (5%)
    pallas_call x1, Pallas kernels, serve(): pl.pallas_call(functools.partial(main_kernel, n, tps), out_shape=(jax.Sha...  141 us
    unnamed x4, local copies, waits for them, and re-layouts  7.65 us

profile of v3, /device:TPU:1, one launch (start us, length us, event | category | flops | bytes accessed | tf_op | source)
XLA Modules:
  0.0 148.8 jit_solution(13728790414482270419)
XLA Ops:
  0.6 1.4 copy.15.table
  2.0 140.5 %serve.1 = (bf16[64,896]{1,0:T(8,128)(2,1)}, bf16[64,896]{1,0:T(8,128)(2,1)}, bf16[64,64,256]{2,1,0:T(8,128)(2,1)}) custom-call(s32[64,4]{1,0:T(8,128)} %copy.15.table, s32[64]{0:T(128)} %lens.1, bf16[64,896]{1,0:T(8,128)(2,1)} %q_ref.1, s32[16,128]{1,0:T(8,128)} %bitcast.4, s32[16,128]{1,0:T(8,128)} %bitcast.5, s32[1,32]{1,0:T(1,128)} %sizes.1, ...), custom_call_target="tpu_custom_call" | custom-call | tf_op jit(solution)/shard_map/serve/pallas_call | solution.py:474
  142.6 1.6 %copy.19 = bf16[64,896]{1,0:T(8,128)(2,1)} copy(bf16[64,896]{1,0:T(8,128)(2,1)} %get-tuple-element.6) | data formatting | bytes 229376
  144.1 1.6 %copy.20 = bf16[64,896]{1,0:T(8,128)(2,1)} copy(bf16[64,896]{1,0:T(8,128)(2,1)} %get-tuple-element.7) | data formatting | bytes 229376
  145.7 3.2 %copy.21 = bf16[64,64,256]{2,1,0:T(8,128)(2,1)} copy(bf16[64,64,256]{2,1,0:T(8,128)(2,1)} %get-tuple-element.8) | data formatting | bytes 4194304

commit v4 on v3

--- a/solution.py
+++ b/solution.py
@@ -121,6 +121,10 @@
     return jnp.concatenate([top, tail], axis=0).astype(jnp.int32)
 
 
+def apart(p, n):
+    return 2 * lax.rem(p, n // 2) + p // (n // 2)
+
+
 def chain_plan(n, reqs, sizes, holder, slot, me):
     segs = sizes.shape[1]
     rows = n * 8
@@ -128,20 +132,27 @@
     tri = before(LANES, segs)
     mine = ones(holder == me)
     order = mm(mine, tri)
-    spread = iota((rows, holder.shape[0]), 0) // (8 * blocks) == iota((rows, holder.shape[0]), 1)
+
+    def sender(number):
+        return lax.rem(me - apart(number // 8, n) + n, n)
+
+    wide = (rows, holder.shape[0])
+    spread = sender(iota(wide, 0)) // blocks == iota(wide, 1)
     y = []
     for q in range(2):
         x = jnp.where((mine > 0.5) & (jnp.abs(order - q) < 0.5), slot, 0).astype(jnp.float32)
         y.append(mm(ones(spread), x))
     number = iota((rows, LANES), 0)
     pick = jnp.where(lax.rem(number // 4, 2) == 0, y[0], y[1])
-    pick = jnp.where(iota((rows, LANES), 1) // segs == lax.rem(number // 8, blocks), pick, 0.0)
+    pick = jnp.where(iota((rows, LANES), 1) // segs == lax.rem(sender(number), blocks), pick, 0.0)
     held = jnp.sum(pick, axis=1, keepdims=True).astype(jnp.int32)
 
     own = row_of(holder, me // blocks)
     hot = ones(iota((n, LANES), 0) == own)
     rank = jnp.sum(hot * mm(hot, tri), axis=0, keepdims=True)
-    value = (own.astype(jnp.float32) * 2 + rank) * SEGMAX
+    away = lax.rem(own - me + n, n)
+    block = lax.rem(away, 2) * (n // 2) + away // 2
+    value = (block.astype(jnp.float32) * 2 + rank) * SEGMAX
     diag = iota((segs, LANES), 1) == lax.rem(me, blocks) * segs + iota((segs, LANES), 0)
     value = jnp.sum(jnp.where(diag, value, 0.0), axis=1, keepdims=True)
     size = sizes.astype(jnp.float32)
@@ -169,16 +180,18 @@
 
 def main_kernel(
     n, tps,
-    table, lens, q_ref, source, wanted, sizes, holder, slot, resident, swap, down_in, up_in,
-    out_ref, delta_ref, arrived,
+    table, lens, q_in, source_in, wanted_in, sizes_in, holder_in, slot_in,
+    resident, swap, down_in, up_in,
+    mixed, delta_ref, arrived,
+    q_ref, source, wanted, sizes, holder, slot, out_ref, ret,
     space, store, near_up, near_down, next_up, next_down, on_up, on_down, third_up, third_down,
-    fourth, crossing, arr, qs, att, down, up, send, got, back, fin, part, parts, plan, book,
+    fourth, crossing, arr, qs, att, down, up, send, got, back, part, parts, plan, book,
     load, s1, r1, s2, r2, s3, r3, s4, r4, sx, rx, ss, rs, sb, rb, st, rt,
 ):
     reqs, width = q_ref.shape
     heads = width // HD
     pool, page = resident.shape[0], resident.shape[1]
-    maxp = table.shape[1]
+    maxp = table.shape[0]
     news = arr.shape[0]
     pages = store.shape[0]
     slots, rank = down.shape[0], down.shape[1]
@@ -195,7 +208,22 @@
         pltpu.make_async_copy(down_in, down, load.at[2]),
         pltpu.make_async_copy(up_in, up, load.at[3]),
     ]
+    small = [
+        pltpu.make_async_copy(a, b, load.at[4 + i])
+        for i, (a, b) in enumerate(
+            (
+                (source_in, source),
+                (wanted_in, wanted),
+                (sizes_in, sizes),
+                (holder_in, holder),
+                (slot_in, slot),
+                (q_in, q_ref),
+            )
+        )
+    ]
     loads[0].start()
+    for copy in small:
+        copy.start()
 
     def hello(d, c):
         pl.semaphore_signal(
@@ -248,6 +276,8 @@
     for copy in loads[1:]:
         copy.start()
 
+    for copy in small:
+        copy.wait()
     plan[...] = ring_plan(source[...], wanted[...], zi, xi, n, pages, news)
     enter = pltpu.make_async_copy(plan, book, load.at[0])
     enter.start()
@@ -336,7 +366,7 @@
     step = 8
 
     def page_at(r, k):
-        t = table[r, k]
+        t = table[k, r]
         return jnp.where(t < pool, jnp.clip(t, 0, pool - 1), spot(jnp.clip(t - pool, 0, news - 1)))
 
     def body(b, c):
@@ -369,91 +399,141 @@
     for h in range(heads):
         out_ref[:, h * HD : (h + 1) * HD] = att[pl.ds(h, reqs, stride=8), :].astype(jnp.bfloat16)
 
+    keep_mixed = pltpu.make_async_copy(out_ref, mixed, load.at[1])
+    keep_mixed.start()
     g = jnp.dot(put, out_ref[...], preferred_element_type=jnp.float32)
     zero = jnp.zeros((8, LANES), jnp.float32)
-
-    def go(src, dst, s_sem, r_sem):
-        def start(d, c):
-            to = lax.rem(me + d, n)
-            pltpu.make_async_remote_copy(
-                src_ref=src.at[to], dst_ref=dst.at[me], send_sem=s_sem.at[d], recv_sem=r_sem.at[d],
-                device_id={"req": to}, device_id_type=MESH,
-            ).start()
+    groups = 2
+    blocks = n // groups
+    group_rows = blocks * 8
+
+    def there(p):
+        to = lax.rem(me + apart(p, n), n)
+        return hop(send.at[p], got.at[p], ss.at[p], rs.at[p], to)
+
+    def home(p):
+        to = lax.rem(me - apart(p, n) + n, n)
+        return hop(ret.at[p], back.at[p], sb.at[p], rb.at[p], to)
+
+    def each(group, act):
+        def one(p, c):
+            act(p)
             return c
 
-        lax.fori_loop(1, n, start, 0)
-
-    def finish(src, dst, s_sem, r_sem):
-        def wait(d, c):
-            to = lax.rem(me + d, n)
-            frm = lax.rem(me + n - d, n)
-            pltpu.make_async_remote_copy(
-                src_ref=src.at[to], dst_ref=dst.at[frm], send_sem=s_sem.at[d], recv_sem=r_sem.at[d],
-                device_id={"req": to}, device_id_type=MESH,
-            ).wait()
-            return c
-
-        lax.fori_loop(1, n, wait, 0)
-
-    for d in range(n):
-        block = [g[d * 8 : (d + 1) * 8, h * HD : (h + 1) * HD] for h in range(heads)]
-        block += [zero] * (8 - heads)
-        send[d] = jnp.concatenate(block, axis=0).astype(jnp.bfloat16)
-    go(send, got, ss, rs)
-    got[me] = send[me]
-    finish(send, got, ss, rs)
-
-    a = by_heads(got[...].astype(jnp.float32), rows, heads).astype(jnp.bfloat16)
-    lane = lax.broadcasted_iota(jnp.int32, (rows, LANES), 1)
+        lax.fori_loop(max(1, group * blocks), (group + 1) * blocks, one, 0)
+
+    for group in range(groups):
+        for p in range(group * blocks, (group + 1) * blocks):
+            block = [g[p * 8 : (p + 1) * 8, h * HD : (h + 1) * HD] for h in range(heads)]
+            block += [zero] * (8 - heads)
+            send[p] = jnp.concatenate(block, axis=0).astype(jnp.bfloat16)
+        each(group, lambda p: there(p).start())
+    got[0] = send[0]
+
+    lane = iota((group_rows, LANES), 1)
     per = LANES // rank
-    total = jnp.zeros((rows, LANES), jnp.float32)
-    for c in range(slots // per):
-        w = down[c * per : (c + 1) * per].reshape(per * rank, width)
-        s = lax.dot_general(a, w, (((1,), (1,)), ((), ())), preferred_element_type=jnp.float32)
-        total = total + jnp.where(hs == c * per + lane // rank, s, 0.0)
-    total = total + pltpu.roll(total, rank, 1)
-    half = rows // 2
-    low = lax.broadcasted_iota(jnp.int32, (half, LANES), 1) < rank
-    part[...] = jnp.where(low, total[:half], total[half:])
-    copies = []
-    for d in range(1, tps):
-        copies.append(
-            pltpu.make_async_remote_copy(
-                src_ref=part, dst_ref=parts.at[d - 1], send_sem=st.at[d - 1], recv_sem=rt.at[d - 1],
-                device_id={"tp": lax.rem(tp + d, tps)}, device_id_type=MESH,
-            )
-        )
-        copies[-1].start()
-    for copy in copies:
-        copy.wait()
-    acc = part[...]
-    for d in range(tps - 1):
-        acc = acc + parts[d]
-    turned = pltpu.roll(acc, rank, 1)
-    shrunk = jnp.concatenate(
-        [jnp.where(low, acc, turned), jnp.where(low, turned, acc)], axis=0
-    ).astype(jnp.bfloat16)
-    spread = jnp.concatenate(
-        [
-            jnp.where(hs == c * per + lane // rank, shrunk, jnp.zeros((), jnp.bfloat16))
-            for c in range(slots // per)
-        ],
-        axis=1,
-    )
-    for h in range(heads):
-        w = up[:, :, h * HD : (h + 1) * HD].reshape(slots * rank, HD)
-        t = jnp.dot(spread, w, preferred_element_type=jnp.float32) * low_rank_scale
-        fin[:, h * 8 : (h + 1) * 8, :] = t.reshape(n, 8, LANES)
-    fin[:, heads * 8 :, :] = jnp.zeros((n, 64 - heads * 8, LANES), jnp.float32)
-    send[...] = fin[...].astype(jnp.bfloat16)
-    go(send, back, sb, rb)
-    back[me] = send[me]
-    finish(send, back, sb, rb)
+    half = group_rows // 2
+    low = iota((half, LANES), 1) < rank
+    exchange = []
+    for group in range(groups):
+        exchange.append(
+            [
+                pltpu.make_async_remote_copy(
+                    src_ref=part.at[group], dst_ref=parts.at[group, d - 1],
+                    send_sem=st.at[group, d - 1], recv_sem=rt.at[group, d - 1],
+                    device_id={"tp": lax.rem(tp + d, tps)}, device_id_type=MESH,
+                )
+                for d in range(1, tps)
+            ]
+        )
+    held = []
+    for group in range(groups):
+        each(group, lambda p: there(p).wait_recv())
+        mine = slice(group * blocks, (group + 1) * blocks)
+        a = by_heads(got[mine].astype(jnp.float32), group_rows, heads).astype(jnp.bfloat16)
+        held.append(hs[group * group_rows : (group + 1) * group_rows])
+        total = jnp.zeros((group_rows, LANES), jnp.float32)
+        for c in range(0, slots, 2 * per):
+            w = down[c : c + 2 * per].reshape(2 * per * rank, width)
+            s = mmt(a, w)
+            total = total + jnp.where(held[group] == c + lane // rank, s[:, :LANES], 0.0)
+            total = total + jnp.where(held[group] == c + per + lane // rank, s[:, LANES:], 0.0)
+        total = total + pltpu.roll(total, rank, 1)
+        part[group] = jnp.where(low, total[:half], total[half:])
+        for copy in exchange[group]:
+            copy.start()
+    for group in range(groups):
+        for copy in exchange[group]:
+            copy.wait_recv()
+        acc = part[group]
+        for d in range(tps - 1):
+            acc = acc + parts[group, d]
+        turned = pltpu.roll(acc, rank, 1)
+        shrunk = jnp.concatenate(
+            [jnp.where(low, acc, turned), jnp.where(low, turned, acc)], axis=0
+        ).astype(jnp.bfloat16)
+        spread = jnp.concatenate(
+            [
+                jnp.where(held[group] == c + lane // rank, shrunk, jnp.zeros((), jnp.bfloat16))
+                for c in range(0, slots, per)
+            ],
+            axis=1,
+        )
+        t = mm(spread, up[...].reshape(slots * rank, width)) * low_rank_scale
+        for p in range(blocks):
+            block = [t[p * 8 : (p + 1) * 8, h * HD : (h + 1) * HD] for h in range(heads)]
+            block += [zero] * (8 - heads)
+            ret[group * blocks + p] = jnp.concatenate(block, axis=0).astype(jnp.bfloat16)
+        each(group, lambda p: home(p).start())
+    back[0] = ret[0]
+    for group in range(groups):
+        each(group, lambda p: there(p).wait_send())
+        for copy in exchange[group]:
+            copy.wait_send()
+    keep.wait()
+    keep_mixed.wait()
+    for group in range(groups):
+        each(group, lambda p: home(p).wait_recv())
     b = by_heads(back[...].astype(jnp.float32), rows, heads).astype(jnp.bfloat16)
     delta_ref[...] = lax.dot_general(
         put, b, (((0,), (0,)), ((), ())), preferred_element_type=jnp.float32
     ).astype(jnp.bfloat16)
-    keep.wait()
+    for group in range(groups):
+        each(group, lambda p: home(p).wait_send())
+
+
+def leave_kernel(count, parts, *refs):
+    ins, outs, held, sems = refs[:count], refs[count : 2 * count], refs[2 * count : 3 * count], refs[-1]
+    into, out = [], []
+    for i in range(count):
+        rows = ins[i].shape[0] // parts[i]
+        for c in range(parts[i]):
+            span = pl.ds(c * rows, rows)
+            at = len(into)
+            into.append(pltpu.make_async_copy(ins[i].at[span], held[i].at[span], sems.at[0, at]))
+            out.append(pltpu.make_async_copy(held[i].at[span], outs[i].at[span], sems.at[1, at]))
+    for copy in into:
+        copy.start()
+    for a, b in zip(into, out):
+        a.wait()
+        b.start()
+    for copy in out:
+        copy.wait()
+
+
+def leave(*arrays):
+    count = len(arrays)
+    parts = [8 if a.ndim == 3 else 1 for a in arrays]
+    hbm = pl.BlockSpec(memory_space=pl.ANY)
+    return pl.pallas_call(
+        functools.partial(leave_kernel, count, parts),
+        out_shape=tuple(jax.ShapeDtypeStruct(a.shape, a.dtype) for a in arrays),
+        in_specs=[hbm] * count,
+        out_specs=(hbm,) * count,
+        scratch_shapes=[pltpu.VMEM(a.shape, a.dtype) for a in arrays]
+        + [pltpu.SemaphoreType.DMA((2, sum(parts)))],
+        name="leave",
+    )(*arrays)
 
 
 def serve(n, tps, table, lens, queries, source, wanted, sizes, holder, slot, resident, swap, down, up):
@@ -478,9 +558,17 @@
             jax.ShapeDtypeStruct((reqs, width), bf16),
             jax.ShapeDtypeStruct((news, page, kvw), bf16),
         ),
-        in_specs=[smem] * 2 + [vmem] * 6 + [hbm] * 4,
-        out_specs=(vmem, vmem, hbm),
+        in_specs=[smem] * 2 + [hbm] * 10,
+        out_specs=(hbm, vmem, hbm),
         scratch_shapes=[
+            pltpu.VMEM(queries.shape, bf16),
+            pltpu.VMEM(source.shape, jnp.int32),
+            pltpu.VMEM(wanted.shape, jnp.int32),
+            pltpu.VMEM(sizes.shape, jnp.int32),
+            pltpu.VMEM(holder.shape, jnp.int32),
+            pltpu.VMEM(slot.shape, jnp.int32),
+            pltpu.VMEM(queries.shape, bf16),
+            pltpu.VMEM((n, 64, LANES), bf16),
             held(pool + n * CAP),
             held(stores), held(stores), held(stores), held(stores), held(stores),
             held(NEAR), held(NEAR), held(NEAR), held(NEAR), held(2 * FAR),
@@ -493,18 +581,17 @@
             pltpu.VMEM((n, 64, LANES), bf16),
             pltpu.VMEM((n, 64, LANES), bf16),
             pltpu.VMEM((n, 64, LANES), bf16),
-            pltpu.VMEM((n, 64, LANES), f32),
-            pltpu.VMEM((rows // 2, LANES), f32),
-            pltpu.VMEM((tps - 1, rows // 2, LANES), f32),
+            pltpu.VMEM((2, rows // 4, LANES), f32),
+            pltpu.VMEM((2, tps - 1, rows // 4, LANES), f32),
             pltpu.VMEM((16 + stores, LANES), jnp.int32),
             pltpu.SMEM((16 + stores, LANES), jnp.int32),
-            dma((4,)),
+            dma((10,)),
             dma((2, stores // CHUNK)), dma((2, stores // CHUNK)),
             dma((2, stores // CHUNK)), dma((2, stores // CHUNK)),
             dma((2, NEAR // CHUNK)), dma((2, NEAR // CHUNK)), dma((2,)), dma((2,)),
             dma((RZ, RX - 1)), dma((RZ, RX - 1)),
             dma((n,)), dma((n,)), dma((n,)), dma((n,)),
-            dma((tps - 1,)), dma((tps - 1,)),
+            dma((2, tps - 1)), dma((2, tps - 1)),
         ],
         compiler_params=pltpu.CompilerParams(
             collective_id=0, has_side_effects=True, vmem_limit_bytes=56 << 20
@@ -527,10 +614,10 @@
     adapter_down,
     adapter_up,
 ):
-    return serve(
+    results = serve(
         lax.axis_size("req"),
         lax.axis_size("tp"),
-        page_table,
+        page_table.T,
         lengths,
         queries,
         resume_source.reshape(-1, LANES),
@@ -543,6 +630,8 @@
         adapter_down,
         adapter_up,
     )
+    mixed, delta, arrived = results
+    return leave(mixed, delta, arrived)
 
 
 def solution(mesh):

time: 149 us -> 139 us (0.933)
  local copies, waits for them, and re-layouts: 7.65 us -> 0 us
  Pallas kernels: 141 us -> 138 us
    unnamed x4 -> x0, local copies, waits for them, and re-layouts: 7.65 us -> none
    pallas_call x1, Pallas kernels: 141 us -> 136 us  [serve(): pl.pallas_call(functools.partial(main_kernel, n, tps), out_shape=(jax.Sha...]
    pallas_call x0 -> x1, Pallas kernels: none -> 2.55 us  [leave(): pl.pallas_call(functools.partial(leave_kernel, count, parts), out_shape=t...]
where the time goes in v4:
time: 139 us
  Pallas kernels  138 us (99%)
    pallas_call x1, Pallas kernels, serve(): pl.pallas_call(functools.partial(main_kernel, n, tps), out_shape=(jax.Sha...  136 us

profile of v4, /device:TPU:1, one launch (start us, length us, event | category | flops | bytes accessed | tf_op | source)
XLA Modules:
  0.0 138.9 jit_solution(4746251832847579166)
XLA Ops:
  0.6 135.7 %serve.1 = (bf16[64,896]{1,0:T(8,128)(2,1)}, bf16[64,896]{1,0:T(8,128)(2,1)}, bf16[64,64,256]{2,1,0:T(8,128)(2,1)}) custom-call(s32[4,64]{1,0:T(4,128)} %bitcast.9, s32[64]{0:T(128)} %lens.1, bf16[64,896]{1,0:T(8,128)(2,1)} %q_in.1, s32[16,128]{1,0:T(8,128)} %bitcast.5, s32[16,128]{1,0:T(8,128)} %bitcast.6, s32[1,32]{1,0:T(1,128)} %sizes_in.1, ...), custom_call_target="tpu_custom_call" | custom-call | tf_op jit(solution)/shard_map/serve/pallas_call | solution.py:554
  136.3 2.5 %leave.1 = (bf16[64,896]{1,0:T(8,128)(2,1)}, bf16[64,896]{1,0:T(8,128)(2,1)}, bf16[64,64,256]{2,1,0:T(8,128)(2,1)}) custom-call(bf16[64,896]{1,0:T(8,128)(2,1)} %get-tuple-element.6.refs_0_, bf16[64,896]{1,0:T(8,128)(2,1)} %get-tuple-element.7.refs_1_, bf16[64,64,256]{2,1,0:T(8,128)(2,1)} %get-tuple-element.8.refs_2_), custom_call_target="tpu_custom_call" | custom-call | tf_op jit(solution)/shard_map/leave/pallas_call | solution.py:528

commit v5 on v4

--- a/solution.py
+++ b/solution.py
@@ -17,6 +17,7 @@
 CHUNK = 8
 NEAR = 24
 FAR = 8
+GROUPS = 4
 
 low_rank_scale = 2.0
 
@@ -56,32 +57,41 @@
 def ring_plan(source, wanted, zi, xi, stores, pages, per_block):
     shape = (RZ, pages)
     zs = iota(shape, 0)
-    need = []
+    need, need_even = [], []
     for zd in range(RZ):
         total = jnp.zeros(shape, jnp.float32)
+        even = jnp.zeros(shape, jnp.float32)
         for h in range(2):
             s = source[2 * zd + h : 2 * zd + h + 1]
             w = wanted[2 * zd + h : 2 * zd + h + 1]
             a = ones(iota((RZ, LANES), 0) * RX + xi == s)
             b = ones(iota((pages, LANES), 0) == w)
             total = total + mmt(a, b)
+            x = 2 * h + iota((RZ, LANES), 1) // per_block
+            even = even + mmt(a * ones(lax.rem(x - xi + RX, 2) == 0), b)
         need.append(total)
-    at = {}
-    for k in (3, 4, 5):
-        at[k] = jnp.zeros(shape, jnp.float32)
+        need_even.append(even)
+
+    def wants(needed, k):
+        found = jnp.zeros(shape, jnp.float32)
         for zd in range(RZ):
-            at[k] = jnp.where(lax.rem(zd - zs + RZ, RZ) == k, need[zd], at[k])
-        at[k] = ones(at[k] > 0.5)
+            found = jnp.where(lax.rem(zd - zs + RZ, RZ) == k, needed[zd], found)
+        return ones(found > 0.5)
+
+    at = {k: wants(need, k) for k in (3, 4, 5)}
+    at_even = {k: wants(need_even, k) for k in (3, 5)}
     tri = before(pages, pages)
     far = at[4]
     far_up = far * ones(mm(far, tri) < FAR - 0.5)
     far_down = far - far_up
     lists = {}
-    for name, f4, f3 in (("up", far_up, at[3]), ("down", far_down, at[5])):
-        f3 = f3 * (1.0 - f4)
+    for name, f4, k in (("up", far_up, 3), ("down", far_down, 5)):
+        f3 = at[k] * (1.0 - f4)
+        half = at_even[k] * f3
+        other = f3 - half
         place4 = mm(f4, tri)
-        place3 = jnp.sum(f4, axis=1, keepdims=True) + mm(f3, tri)
-        lists[name] = (f4, f3, place4, f4 * place4 + f3 * place3)
+        place3 = half * (FAR + mm(half, tri)) + other * (NEAR - CHUNK + mm(other, tri))
+        lists[name] = (f4, f3, place4, f4 * place4 + place3)
     page_id = iota(shape, 1).astype(jnp.float32)
     k = lax.rem(zi - zs + RZ, RZ)
     spot4 = jnp.where(far_up > 0.5, lists["up"][2], FAR + lists["down"][2])
@@ -122,7 +132,7 @@
 
 
 def apart(p, n):
-    return 2 * lax.rem(p, n // 2) + p // (n // 2)
+    return GROUPS * lax.rem(p, n // GROUPS) + p // (n // GROUPS)
 
 
 def chain_plan(n, reqs, sizes, holder, slot, me):
@@ -151,7 +161,7 @@
     hot = ones(iota((n, LANES), 0) == own)
     rank = jnp.sum(hot * mm(hot, tri), axis=0, keepdims=True)
     away = lax.rem(own - me + n, n)
-    block = lax.rem(away, 2) * (n // 2) + away // 2
+    block = lax.rem(away, GROUPS) * (n // GROUPS) + away // GROUPS
     value = (block.astype(jnp.float32) * 2 + rank) * SEGMAX
     diag = iota((segs, LANES), 1) == lax.rem(me, blocks) * segs + iota((segs, LANES), 0)
     value = jnp.sum(jnp.where(diag, value, 0.0), axis=1, keepdims=True)
@@ -185,6 +195,7 @@
     mixed, delta_ref, arrived,
     q_ref, source, wanted, sizes, holder, slot, out_ref, ret,
     space, store, near_up, near_down, next_up, next_down, on_up, on_down, third_up, third_down,
+    rest_up, rest_down, all_up, all_down,
     fourth, crossing, arr, qs, att, down, up, send, got, back, part, parts, plan, book,
     load, s1, r1, s2, r2, s3, r3, s4, r4, sx, rx, ss, rs, sb, rb, st, rt,
 ):
@@ -249,6 +260,8 @@
     near, nxt, on, third = (
         (near_up, near_down), (next_up, next_down), (on_up, on_down), (third_up, third_down)
     )
+    rest, whole = (rest_up, rest_down), (all_up, all_down)
+    early = NEAR // CHUNK - 1
 
     def part_of(ref, c):
         return ref.at[pl.ds(c * CHUNK, CHUNK)]
@@ -264,9 +277,8 @@
             )
     for c in range(NEAR // CHUNK):
         for w in range(2):
-            later.append(
-                hop(part_of(on[w], c), part_of(third[w], c), s3.at[w, c], r3.at[w, c], sides[w])
-            )
+            to = part_of(third[w], c) if c < early else rest[w]
+            later.append(hop(part_of(on[w], c), to, s3.at[w, c], r3.at[w, c], sides[w]))
     for w in range(2):
         last.append(
             hop(third[w].at[pl.ds(0, FAR)], part_of(fourth, w), s4.at[w], r4.at[w], sides[w])
@@ -304,15 +316,17 @@
     def z_row(dx):
         return zi * RX + lax.rem(xi + dx, RX)
 
-    def cross(k, ref):
+    def cross(k, ref, ways=(2, 1, 3, 0)):
         z = lax.rem(zi + RZ - k, RZ)
-        for dx in (2, 1, 3):
+        for dx in ways:
+            if dx == 0:
+                for r in range(CAP):
+                    space[land(z, xi) + r] = ref[within(book[z, xi * CAP + r], ref)]
+                continue
             xd = lax.rem(xi + dx, RX)
             for r in range(CAP):
                 crossing[k, dx - 1, r] = ref[within(book[z, xd * CAP + r], ref)]
             cross_copy(k, dx).start()
-        for r in range(CAP):
-            space[land(z, xi) + r] = ref[within(book[z, xi * CAP + r], ref)]
 
     cross(0, store)
     for a, b in zip(first, second):
@@ -329,22 +343,27 @@
             later[c * 2 + w].start()
     cross(2, next_up)
     cross(6, next_down)
-    for i, copy in enumerate(later):
+    for i, copy in enumerate(later[: 2 * early]):
         copy.wait_recv()
         if i < 2:
             last[i].start()
-    cross(3, third_up)
-    cross(5, third_down)
+    cross(3, third_up, (2, 0))
+    cross(5, third_down, (2, 0))
+    for w in range(2):
+        whole[w][pl.ds(0, early * CHUNK)] = third[w][...]
+    for copy in later[2 * early :]:
+        copy.wait_recv()
+    for w in range(2):
+        whole[w][pl.ds(early * CHUNK, CHUNK)] = rest[w][...]
+    cross(3, all_up, (1, 3))
+    cross(5, all_down, (1, 3))
     for copy in last:
         copy.wait_recv()
     cross(4, fourth)
     for copy in loads[1:]:
         copy.wait()
-    for copy in first + second + later + last:
-        copy.wait_send()
     for k in range(RZ):
         for dx in range(1, RX):
-            cross_copy(k, dx).wait_send()
             z = lax.rem(zi + RZ - k, RZ)
             x = lax.rem(xi + RX - dx, RX)
             hop(
@@ -355,15 +374,7 @@
     def spot(j):
         return pool + jnp.clip(book[8 + xi // 2, lax.rem(xi, 2) * news + j], 0, n * CAP - 1)
 
-    def pick(j, c):
-        arr[j] = space[spot(j)]
-        return c
-
-    lax.fori_loop(0, news, pick, 0)
-    keep = pltpu.make_async_copy(arr, arrived, load.at[0])
-    keep.start()
-
-    step = 8
+    step = 16
 
     def page_at(r, k):
         t = table[k, r]
@@ -403,7 +414,7 @@
     keep_mixed.start()
     g = jnp.dot(put, out_ref[...], preferred_element_type=jnp.float32)
     zero = jnp.zeros((8, LANES), jnp.float32)
-    groups = 2
+    groups = GROUPS
     blocks = n // groups
     group_rows = blocks * 8
 
@@ -446,12 +457,12 @@
                 for d in range(1, tps)
             ]
         )
-    held = []
-    for group in range(groups):
+    held = [hs[group * group_rows : (group + 1) * group_rows] for group in range(groups)]
+
+    def shrink(group):
         each(group, lambda p: there(p).wait_recv())
         mine = slice(group * blocks, (group + 1) * blocks)
         a = by_heads(got[mine].astype(jnp.float32), group_rows, heads).astype(jnp.bfloat16)
-        held.append(hs[group * group_rows : (group + 1) * group_rows])
         total = jnp.zeros((group_rows, LANES), jnp.float32)
         for c in range(0, slots, 2 * per):
             w = down[c : c + 2 * per].reshape(2 * per * rank, width)
@@ -462,7 +473,8 @@
         part[group] = jnp.where(low, total[:half], total[half:])
         for copy in exchange[group]:
             copy.start()
-    for group in range(groups):
+
+    def expand(group):
         for copy in exchange[group]:
             copy.wait_recv()
         acc = part[group]
@@ -485,11 +497,32 @@
             block += [zero] * (8 - heads)
             ret[group * blocks + p] = jnp.concatenate(block, axis=0).astype(jnp.bfloat16)
         each(group, lambda p: home(p).start())
+
+    def pick(j, c):
+        arr[j] = space[spot(j)]
+        return c
+
+    lax.fori_loop(0, news, pick, 0)
+    keep = pltpu.make_async_copy(arr, arrived, load.at[0])
+    keep.start()
+    shrink(0)
+    shrink(1)
+    expand(0)
+    shrink(2)
+    expand(1)
+    shrink(3)
+    expand(2)
+    expand(3)
     back[0] = ret[0]
     for group in range(groups):
         each(group, lambda p: there(p).wait_send())
         for copy in exchange[group]:
             copy.wait_send()
+    for copy in first + second + later + last:
+        copy.wait_send()
+    for k in range(RZ):
+        for dx in range(1, RX):
+            cross_copy(k, dx).wait_send()
     keep.wait()
     keep_mixed.wait()
     for group in range(groups):
@@ -571,7 +604,8 @@
             pltpu.VMEM((n, 64, LANES), bf16),
             held(pool + n * CAP),
             held(stores), held(stores), held(stores), held(stores), held(stores),
-            held(NEAR), held(NEAR), held(NEAR), held(NEAR), held(2 * FAR),
+            held(NEAR), held(NEAR), held(NEAR - CHUNK), held(NEAR - CHUNK), held(CHUNK), held(CHUNK),
+            held(NEAR), held(NEAR), held(2 * FAR),
             pltpu.VMEM((RZ, RX - 1, CAP, page, kvw), bf16),
             held(news),
             pltpu.VMEM((reqs * 8, LANES), f32),
@@ -581,8 +615,8 @@
             pltpu.VMEM((n, 64, LANES), bf16),
             pltpu.VMEM((n, 64, LANES), bf16),
             pltpu.VMEM((n, 64, LANES), bf16),
-            pltpu.VMEM((2, rows // 4, LANES), f32),
-            pltpu.VMEM((2, tps - 1, rows // 4, LANES), f32),
+            pltpu.VMEM((GROUPS, rows // (2 * GROUPS), LANES), f32),
+            pltpu.VMEM((GROUPS, tps - 1, rows // (2 * GROUPS), LANES), f32),
             pltpu.VMEM((16 + stores, LANES), jnp.int32),
             pltpu.SMEM((16 + stores, LANES), jnp.int32),
             dma((10,)),
@@ -591,7 +625,7 @@
             dma((2, NEAR // CHUNK)), dma((2, NEAR // CHUNK)), dma((2,)), dma((2,)),
             dma((RZ, RX - 1)), dma((RZ, RX - 1)),
             dma((n,)), dma((n,)), dma((n,)), dma((n,)),
-            dma((2, tps - 1)), dma((2, tps - 1)),
+            dma((GROUPS, tps - 1)), dma((GROUPS, tps - 1)),
         ],
         compiler_params=pltpu.CompilerParams(
             collective_id=0, has_side_effects=True, vmem_limit_bytes=56 << 20

time: 139 us -> 130 us (0.935)
  Pallas kernels: 138 us -> 129 us
    pallas_call x1, Pallas kernels: 136 us -> 126 us  [serve(): pl.pallas_call(functools.partial(main_kernel, n, tps), out_shape=(jax.Sha...]
where the time goes in v5:
time: 130 us
  Pallas kernels  129 us (99%)
    pallas_call x1, Pallas kernels, serve(): pl.pallas_call(functools.partial(main_kernel, n, tps), out_shape=(jax.Sha...  126 us

profile of v5, /device:TPU:1, one launch (start us, length us, event | category | flops | bytes accessed | tf_op | source)
XLA Modules:
  0.0 129.7 jit_solution(15879034891976391838)
XLA Ops:
  0.6 126.5 %serve.1 = (bf16[64,896]{1,0:T(8,128)(2,1)}, bf16[64,896]{1,0:T(8,128)(2,1)}, bf16[64,64,256]{2,1,0:T(8,128)(2,1)}) custom-call(s32[4,64]{1,0:T(4,128)} %bitcast.9, s32[64]{0:T(128)} %lens.1, bf16[64,896]{1,0:T(8,128)(2,1)} %q_in.1, s32[16,128]{1,0:T(8,128)} %bitcast.5, s32[16,128]{1,0:T(8,128)} %bitcast.6, s32[1,32]{1,0:T(1,128)} %sizes_in.1, ...), custom_call_target="tpu_custom_call" | custom-call | tf_op jit(solution)/shard_map/serve/pallas_call | solution.py:587
  127.1 2.5 %leave.1 = (bf16[64,896]{1,0:T(8,128)(2,1)}, bf16[64,896]{1,0:T(8,128)(2,1)}, bf16[64,64,256]{2,1,0:T(8,128)(2,1)}) custom-call(bf16[64,896]{1,0:T(8,128)(2,1)} %get-tuple-element.6.refs_0_, bf16[64,896]{1,0:T(8,128)(2,1)} %get-tuple-element.7.refs_1_, bf16[64,64,256]{2,1,0:T(8,128)(2,1)} %get-tuple-element.8.refs_2_), custom_call_target="tpu_custom_call" | custom-call | tf_op jit(solution)/shard_map/leave/pallas_call | solution.py:561

commit v6 on v5

--- a/solution.py
+++ b/solution.py
@@ -190,10 +190,10 @@
 
 def main_kernel(
     n, tps,
-    table, lens, q_in, source_in, wanted_in, sizes_in, holder_in, slot_in,
+    table_in, lens_in, q_in, source_in, wanted_in, sizes_in, holder_in, slot_in,
     resident, swap, down_in, up_in,
     mixed, delta_ref, arrived,
-    q_ref, source, wanted, sizes, holder, slot, out_ref, ret,
+    table, lens, q_ref, source, wanted, sizes, holder, slot, out_ref, ret,
     space, store, near_up, near_down, next_up, next_down, on_up, on_down, third_up, third_down,
     rest_up, rest_down, all_up, all_down,
     fourth, crossing, arr, qs, att, down, up, send, got, back, part, parts, plan, book,
@@ -229,6 +229,8 @@
                 (holder_in, holder),
                 (slot_in, slot),
                 (q_in, q_ref),
+                (table_in, table),
+                (lens_in, lens),
             )
         )
     ]
@@ -336,8 +338,8 @@
     cross(7, near_down)
     for copy in second:
         copy.wait_recv()
-    for w in range(2):
-        for c in range(NEAR // CHUNK):
+    for c in range(NEAR // CHUNK):
+        for w in range(2):
             for i in range(CHUNK):
                 on[w][c * CHUNK + i] = nxt[w][within(book[16 + c * CHUNK + i, w], nxt[w])]
             later[c * 2 + w].start()
@@ -374,7 +376,7 @@
     def spot(j):
         return pool + jnp.clip(book[8 + xi // 2, lax.rem(xi, 2) * news + j], 0, n * CAP - 1)
 
-    step = 16
+    step = 32
 
     def page_at(r, k):
         t = table[k, r]
@@ -574,7 +576,6 @@
     pool, page, kvw = resident.shape
     news = source.size // n
     rows = n * 8
-    smem = pl.BlockSpec(memory_space=pltpu.SMEM)
     vmem = pl.BlockSpec(memory_space=pltpu.VMEM)
     hbm = pl.BlockSpec(memory_space=pl.ANY)
     dma = pltpu.SemaphoreType.DMA
@@ -591,9 +592,11 @@
             jax.ShapeDtypeStruct((reqs, width), bf16),
             jax.ShapeDtypeStruct((news, page, kvw), bf16),
         ),
-        in_specs=[smem] * 2 + [hbm] * 10,
+        in_specs=[hbm] * 12,
         out_specs=(hbm, vmem, hbm),
         scratch_shapes=[
+            pltpu.SMEM(table.shape, jnp.int32),
+            pltpu.SMEM(lens.shape, jnp.int32),
             pltpu.VMEM(queries.shape, bf16),
             pltpu.VMEM(source.shape, jnp.int32),
             pltpu.VMEM(wanted.shape, jnp.int32),
@@ -619,7 +622,7 @@
             pltpu.VMEM((GROUPS, tps - 1, rows // (2 * GROUPS), LANES), f32),
             pltpu.VMEM((16 + stores, LANES), jnp.int32),
             pltpu.SMEM((16 + stores, LANES), jnp.int32),
-            dma((10,)),
+            dma((12,)),
             dma((2, stores // CHUNK)), dma((2, stores // CHUNK)),
             dma((2, stores // CHUNK)), dma((2, stores // CHUNK)),
             dma((2, NEAR // CHUNK)), dma((2, NEAR // CHUNK)), dma((2,)), dma((2,)),

time: 130 us -> 129 us (level)
    pallas_call x1, Pallas kernels: 126 us -> 125 us  [serve(): pl.pallas_call(functools.partial(main_kernel, n, tps), out_shape=(jax.Sha...]
where the time goes in v6:
time: 129 us; the launch traced here: 128 us
  Pallas kernels  128 us (99%)
    pallas_call x1, Pallas kernels, serve(): pl.pallas_call(functools.partial(main_kernel, n, tps), out_shape=(jax.Sha...  125 us

profile of v6, /device:TPU:1, one launch (start us, length us, event | category | flops | bytes accessed | tf_op | source)
XLA Modules:
  0.0 128.4 jit_solution(179958654258004280)
XLA Ops:
  0.6 125.2 %serve.1 = (bf16[64,896]{1,0:T(8,128)(2,1)}, bf16[64,896]{1,0:T(8,128)(2,1)}, bf16[64,64,256]{2,1,0:T(8,128)(2,1)}) custom-call(s32[4,64]{1,0:T(4,128)} %bitcast.9, s32[64]{0:T(128)} %lens_in.1, bf16[64,896]{1,0:T(8,128)(2,1)} %q_in.1, s32[16,128]{1,0:T(8,128)} %bitcast.5, s32[16,128]{1,0:T(8,128)} %bitcast.6, s32[1,32]{1,0:T(1,128)} %sizes_in.1, ...), custom_call_target="tpu_custom_call" | custom-call | tf_op jit(solution)/shard_map/serve/pallas_call | solution.py:588
  125.8 2.5 %leave.1 = (bf16[64,896]{1,0:T(8,128)(2,1)}, bf16[64,896]{1,0:T(8,128)(2,1)}, bf16[64,64,256]{2,1,0:T(8,128)(2,1)}) custom-call(bf16[64,896]{1,0:T(8,128)(2,1)} %get-tuple-element.6.refs_0_, bf16[64,896]{1,0:T(8,128)(2,1)} %get-tuple-element.7.refs_1_, bf16[64,64,256]{2,1,0:T(8,128)(2,1)} %get-tuple-element.8.refs_2_), custom_call_target="tpu_custom_call" | custom-call | tf_op jit(solution)/shard_map/leave/pallas_call | solution.py:563
